TPU v7x, 256 devices: a whole 4x4x8 slice. The times are simulated.
256 devices in a mesh: ctx: 128 (over y, z, x), ch: 2 (over core).
Axes of the slice: x: 4, y: 4, z: 8, core: 2. Of those that a mesh axis runs over, the one named last changes fastest.
Arguments:
- query_act: bfloat16 [32768, 512], P('ctx', 'ch'), may hold values from -6 to 6
- key_act: bfloat16 [32768, 512], P('ctx', 'ch'), may hold values from -6 to 6
- value_act: bfloat16 [32768, 512], P('ctx', 'ch'), may hold values from -6 to 6
- filter_taps: float32 [32768, 512], P('ctx', 'ch'), may hold values from -2 to 2
- skip_gain: float32 [512], P('ch'), may hold values from -4 to 4
- out_weight: bfloat16 [512, 512], P('ch'), may hold values from -0.25 to 0.25
- out_grad: bfloat16 [32768, 512], P('ctx', 'ch'), may hold values from -6 to 6
Outputs:
- output: bfloat16 [32768, 512], P('ctx', 'ch')
- grad_query: bfloat16 [32768, 512], P('ctx', 'ch')
- grad_key: bfloat16 [32768, 512], P('ctx', 'ch')
- grad_value: bfloat16 [32768, 512], P('ctx', 'ch')
- grad_filter: float32 [32768, 512], P('ctx', 'ch')
- grad_skip: float32 [512], P('ch')
- grad_out_weight: float32 [512, 512], P('ch')
All inputs are finite; a program needn't handle non-finite values.
Results may differ from a plain program's by a relative error of at most 0.0049.
Values may be sent and summed in bfloat16 or wider, within the bound.
A program may use at most 128 MiB of HBM per device.

v0:
```python
from functools import partial
import math

import jax
import jax.numpy as jnp
from jax import lax
from jax.sharding import PartitionSpec as P

exact_einsum = partial(jnp.einsum, precision=lax.Precision.HIGHEST)


def index_grid(shape, axis_pos):
    return lax.broadcasted_iota(jnp.int32, shape, axis_pos)


def phases(phase_num, period, sign):
    angle = sign * 2.0 * math.pi / period * phase_num.astype(jnp.float32)
    return (jnp.cos(angle), jnp.sin(angle))


def apply_table(form, wave_re, wave_im, sig_re, sig_im):
    out_re = exact_einsum(form, wave_re, sig_re) - exact_einsum(form, wave_im, sig_im)
    out_im = exact_einsum(form, wave_re, sig_im) + exact_einsum(form, wave_im, sig_re)
    return (out_re, out_im)


def twiddle(wave_re, wave_im, sig_re, sig_im):
    return (wave_re * sig_re - wave_im * sig_im, wave_re * sig_im + wave_im * sig_re)


def route_signal(blocks):
    moved_data = lax.all_to_all(blocks, "ctx", split_axis=0, concat_axis=0, tiled=True)
    return moved_data


def route_spectrum(spec_re, spec_im):
    moved_re, moved_im = (
        lax.all_to_all(spec_re, "ctx", split_axis=0, concat_axis=0, tiled=True),
        lax.all_to_all(spec_im, "ctx", split_axis=0, concat_axis=0, tiled=True),
    )
    return (moved_re, moved_im)


def forward_spectrum(signal):
    n_dev = lax.axis_size("ctx")
    my_rank = lax.axis_index("ctx")
    n_rows, n_chan = signal.shape
    per_block = n_rows // n_dev
    total_len = 2 * n_rows * n_dev
    blocks = signal.reshape(n_dev, per_block, n_chan)
    blocks = jnp.stack((blocks, jnp.zeros_like(blocks)), 1)
    arrived = route_signal(blocks)
    shape_q = (2 * n_dev, n_dev, 2)
    phase_num = (
        index_grid(shape_q, 0)
        * (index_grid(shape_q, 2) * n_dev + index_grid(shape_q, 1))
        % (2 * n_dev)
    )
    wave_re, wave_im = phases(phase_num, 2 * n_dev, -1.0)
    spec_re = exact_einsum("kps,psrc->krc", wave_re, arrived)
    spec_im = exact_einsum("kps,psrc->krc", wave_im, arrived)
    shape_t = (2 * n_dev, per_block)
    phase_num = index_grid(shape_t, 0) * (my_rank * per_block + index_grid(shape_t, 1)) % total_len
    wave_re, wave_im = phases(phase_num, total_len, -1.0)
    spec_re, spec_im = twiddle(wave_re[:, :, None], wave_im[:, :, None], spec_re, spec_im)
    spec_re = spec_re.reshape(n_dev, 2, per_block, n_chan)
    spec_im = spec_im.reshape(n_dev, 2, per_block, n_chan)
    spec_re, spec_im = route_spectrum(spec_re, spec_im)
    shape_m = (n_dev, n_dev)
    phase_num = index_grid(shape_m, 0) * index_grid(shape_m, 1) % n_dev
    wave_re, wave_im = phases(phase_num, n_dev, -1.0)
    spec_re, spec_im = apply_table("mj,jtrc->mtrc", wave_re, wave_im, spec_re, spec_im)
    shape_b = (n_dev, per_block)
    phase_num = index_grid(shape_b, 0) * index_grid(shape_b, 1) % n_rows
    wave_re, wave_im = phases(phase_num, n_rows, -1.0)
    spec_re, spec_im = twiddle(
        wave_re[:, None, :, None], wave_im[:, None, :, None], spec_re, spec_im
    )
    shape_n = (per_block, per_block)
    phase_num = index_grid(shape_n, 0) * index_grid(shape_n, 1) % per_block
    wave_re, wave_im = phases(phase_num, per_block, -1.0)
    return apply_table("nr,mtrc->mtnc", wave_re, wave_im, spec_re, spec_im)


def inverse_signal(spec_re, spec_im):
    n_dev = lax.axis_size("ctx")
    my_rank = lax.axis_index("ctx")
    per_block = spec_re.shape[2]
    n_chan = spec_re.shape[3]
    n_rows = per_block * n_dev
    total_len = 2 * n_rows * n_dev
    shape_n = (per_block, per_block)
    phase_num = index_grid(shape_n, 0) * index_grid(shape_n, 1) % per_block
    wave_re, wave_im = phases(phase_num, per_block, 1.0)
    spec_re, spec_im = apply_table("rn,mtnc->mtrc", wave_re, wave_im, spec_re, spec_im)
    shape_b = (n_dev, per_block)
    phase_num = index_grid(shape_b, 0) * index_grid(shape_b, 1) % n_rows
    wave_re, wave_im = phases(phase_num, n_rows, 1.0)
    spec_re, spec_im = twiddle(
        wave_re[:, None, :, None], wave_im[:, None, :, None], spec_re, spec_im
    )
    shape_m = (n_dev, n_dev)
    phase_num = index_grid(shape_m, 0) * index_grid(shape_m, 1) % n_dev
    wave_re, wave_im = phases(phase_num, n_dev, 1.0)
    spec_re, spec_im = apply_table("jm,mtrc->jtrc", wave_re, wave_im, spec_re, spec_im)
    spec_re, spec_im = route_spectrum(spec_re, spec_im)
    spec_re = spec_re.reshape(2 * n_dev, per_block, n_chan)
    spec_im = spec_im.reshape(2 * n_dev, per_block, n_chan)
    shape_t = (2 * n_dev, per_block)
    phase_num = index_grid(shape_t, 0) * (my_rank * per_block + index_grid(shape_t, 1)) % total_len
    wave_re, wave_im = phases(phase_num, total_len, 1.0)
    spec_re, spec_im = twiddle(wave_re[:, :, None], wave_im[:, :, None], spec_re, spec_im)
    shape_q = (n_dev, 2, 2 * n_dev)
    phase_num = (
        (index_grid(shape_q, 1) * n_dev + index_grid(shape_q, 0))
        * index_grid(shape_q, 2)
        % (2 * n_dev)
    )
    wave_re, wave_im = phases(phase_num, 2 * n_dev, 1.0)
    local_out = exact_einsum("psk,krc->psrc", wave_re, spec_re) - exact_einsum(
        "psk,krc->psrc", wave_im, spec_im
    )
    arrived = route_signal(local_out)[:, 0]
    return arrived.reshape(n_rows, n_chan) / total_len


def shards(query_act, key_act, value_act, filter_taps, skip_gain, out_weight, out_grad):
    n_rows, n_chan = query_act.shape
    n_dev = lax.axis_size("ctx")
    root_tokens = math.sqrt(n_rows * n_dev)
    query_f = query_act.astype(jnp.float32)
    key_f = key_act.astype(jnp.float32)
    value_f = value_act.astype(jnp.float32)
    product = key_f * value_f
    spec_re, spec_im = forward_spectrum(jnp.concatenate((product, filter_taps), 1))
    sig_re, sig_im = (spec_re[..., :n_chan], spec_im[..., :n_chan])
    tap_re, tap_im = (spec_re[..., n_chan:], spec_im[..., n_chan:])
    conv_re = sig_re * tap_re - sig_im * tap_im
    conv_im = sig_re * tap_im + sig_im * tap_re
    conv = inverse_signal(conv_re, conv_im)
    mixed_act = conv + skip_gain * product
    gated_act = (query_f * mixed_act).astype(jnp.bfloat16)
    partial_terms = jnp.dot(gated_act, out_weight, preferred_element_type=jnp.float32)
    output = lax.psum_scatter(partial_terms, "ch", scatter_dimension=1, tiled=True).astype(
        jnp.bfloat16
    )
    grad_full = lax.all_gather(out_grad, "ch", axis=1, tiled=True)
    d_gated = lax.dot_general(
        grad_full, out_weight, (((1,), (1,)), ((), ())), preferred_element_type=jnp.float32
    )
    grad_query = (d_gated * mixed_act).astype(jnp.bfloat16)
    d_mixed = d_gated * query_f
    grad_re, grad_im = forward_spectrum(d_mixed)
    back_re = jnp.concatenate(
        (grad_re * tap_re + grad_im * tap_im, grad_re * sig_re + grad_im * sig_im), -1
    )
    back_im = jnp.concatenate(
        (grad_im * tap_re - grad_re * tap_im, grad_im * sig_re - grad_re * sig_im), -1
    )
    lagged = inverse_signal(back_re, back_im)
    lag_product = lagged[:, :n_chan]
    lag_filter = lagged[:, n_chan:]
    grad_product = lag_product + skip_gain * d_mixed
    grad_filter = lag_filter / root_tokens
    grad_key = (grad_product * value_f).astype(jnp.bfloat16)
    grad_value = (grad_product * key_f).astype(jnp.bfloat16)
    weight_part = lax.dot_general(
        gated_act, grad_full, (((0,), (0,)), ((), ())), preferred_element_type=jnp.float32
    )
    skip_part = jnp.sum(d_mixed * product, axis=0)
    weight_sum, skip_sum = lax.psum((weight_part, skip_part), "ctx")
    return (
        output,
        grad_query,
        grad_key,
        grad_value,
        grad_filter,
        skip_sum / root_tokens,
        weight_sum / root_tokens,
    )


def solution(mesh):
    in_specs = (
        P("ctx", "ch"),
        P("ctx", "ch"),
        P("ctx", "ch"),
        P("ctx", "ch"),
        P("ch"),
        P("ch", None),
        P("ctx", "ch"),
    )
    out_specs = (
        P("ctx", "ch"),
        P("ctx", "ch"),
        P("ctx", "ch"),
        P("ctx", "ch"),
        P("ctx", "ch"),
        P("ch"),
        P("ch", None),
    )
    return jax.shard_map(shards, mesh=mesh, in_specs=in_specs, out_specs=out_specs, check_vma=False)
```

profile of v0, /device:TPU:2, one launch (start us, length us, event | category | flops | bytes accessed | tf_op | source)
XLA Modules:
  0.0 772.9 jit_solution(6925120534662040415)
XLA Ops:
  13.7 15.6 %all-to-all-start.6 = ((f32[128,2,2,256]{3,1,2,0:T(2,128)}), f32[128,2,2,256]{3,1,2,0:T(2,128)S(1)}, u32[]{:S(2)}, u32[]{:S(2)}) async-start(f32[128,2,2,256]{3,1,2,0:T(2,128)} %stack.7), calls=%async_computation.7 | async-start | bytes 1048576 | tf_op jit(solution)/shard_map/all_to_all | solution.py:32
  31.4 17.0 %all-to-all-done.6 = f32[128,2,2,256]{3,1,2,0:T(2,128)S(1)} async-done(((f32[128,2,2,256]{3,1,2,0:T(2,128)}), f32[128,2,2,256]{3,1,2,0:T(2,128)S(1)}, u32[]{:S(2)}, u32[]{:S(2)}) %all-to-all-start.6) | async-done | bytes 524320 | tf_op jit(solution)/shard_map/all_to_all | solution.py:32
  48.4 7.5 all-to-all-start
  61.3 23.0 %all-to-all-done = f32[128,2,2,512]{3,1,2,0:T(2,128)S(1)} async-done(((f32[128,2,2,512]{3,1,2,0:T(2,128)}), f32[128,2,2,512]{3,1,2,0:T(2,128)S(1)}, u32[]{:S(2)}, u32[]{:S(2)}) %all-to-all-start) | async-done | bytes 1048608 | tf_op jit(solution)/shard_map/all_to_all | solution.py:32
  84.4 8.1 %all-to-all-start.7 = ((f32[128,2,2,256]{3,2,1,0:T(2,128)}), f32[128,2,2,256]{3,2,1,0:T(2,128)S(1)}, u32[]{:S(2)}, u32[]{:S(2)}) async-start(f32[128,2,2,256]{3,2,1,0:T(2,128)} %bitcast.49), calls=%async_computation.8 | async-start | bytes 1048576 | tf_op jit(solution)/shard_map/all_to_all | solution.py:38
  93.7 15.9 %all-to-all-done.7 = f32[128,2,2,256]{3,2,1,0:T(2,128)S(1)} async-done(((f32[128,2,2,256]{3,2,1,0:T(2,128)}), f32[128,2,2,256]{3,2,1,0:T(2,128)S(1)}, u32[]{:S(2)}, u32[]{:S(2)}) %all-to-all-start.7) | async-done | bytes 524320 | tf_op jit(solution)/shard_map/all_to_all | solution.py:38
  109.6 7.4 all-to-all-start.8
  124.5 9.0 %all-to-all-done.8 = f32[128,2,2,256]{3,2,1,0:T(2,128)S(1)} async-done(((f32[128,2,2,256]{3,2,1,0:T(2,128)}), f32[128,2,2,256]{3,2,1,0:T(2,128)S(1)}, u32[]{:S(2)}, u32[]{:S(2)}) %all-to-all-start.8) | async-done | bytes 524320 | tf_op jit(solution)/shard_map/all_to_all | solution.py:39
  133.5 7.6 all-to-all-start.1
  144.6 22.5 %all-to-all-done.1 = f32[128,2,2,512]{3,2,1,0:T(2,128)S(1)} async-done(((f32[128,2,2,512]{3,2,1,0:T(2,128)}), f32[128,2,2,512]{3,2,1,0:T(2,128)S(1)}, u32[]{:S(2)}, u32[]{:S(2)}) %all-to-all-start.1) | async-done | bytes 1048608 | tf_op jit(solution)/shard_map/all_to_all | solution.py:38
  167.1 8.3 %all-to-all-start.2 = ((f32[128,2,2,512]{3,2,1,0:T(2,128)}), f32[128,2,2,512]{3,2,1,0:T(2,128)S(1)}, u32[]{:S(2)}, u32[]{:S(2)}) async-start(f32[128,2,2,512]{3,2,1,0:T(2,128)} %bitcast.208), calls=%async_computation.2 | async-start | bytes 2097152 | tf_op jit(solution)/shard_map/all_to_all | solution.py:39
  188.5 11.7 %all-to-all-done.2 = f32[128,2,2,512]{3,2,1,0:T(2,128)S(1)} async-done(((f32[128,2,2,512]{3,2,1,0:T(2,128)}), f32[128,2,2,512]{3,2,1,0:T(2,128)S(1)}, u32[]{:S(2)}, u32[]{:S(2)}) %all-to-all-start.2) | async-done | bytes 1048608 | tf_op jit(solution)/shard_map/all_to_all | solution.py:39
  237.8 7.9 %all-to-all-start.3 = ((f32[128,2,2,256]{3,2,1,0:T(2,128)}), f32[128,2,2,256]{3,2,1,0:T(2,128)S(1)}, u32[]{:S(2)}, u32[]{:S(2)}) async-start(f32[128,2,2,256]{3,2,1,0:T(2,128)} %copy.98), calls=%async_computation.3 | async-start | bytes 1048576 | tf_op jit(solution)/shard_map/all_to_all | solution.py:38
  253.3 5.5 convolution_add_fusion.2
  261.8 12.4 %all-to-all-start.4 = ((f32[128,2,2,256]{3,2,1,0:T(2,128)}), f32[128,2,2,256]{3,2,1,0:T(2,128)}, u32[]{:S(2)}, u32[]{:S(2)}) async-start(f32[128,2,2,256]{3,2,1,0:T(2,128)} %copy.102), calls=%async_computation.4 | async-start | bytes 1048576 | tf_op jit(solution)/shard_map/all_to_all | solution.py:39
  288.9 14.1 %all-to-all-start.9 = ((f32[128,2,2,512]{3,2,1,0:T(2,128)}), f32[128,2,2,512]{3,2,1,0:T(2,128)S(1)}, u32[]{:S(2)}, u32[]{:S(2)}) async-start(f32[128,2,2,512]{3,2,1,0:T(2,128)} %copy.124), calls=%async_computation.10 | async-start | bytes 2097152 | tf_op jit(solution)/shard_map/all_to_all | solution.py:38
  307.8 19.0 %all-to-all-done.9 = f32[128,2,2,512]{3,2,1,0:T(2,128)S(1)} async-done(((f32[128,2,2,512]{3,2,1,0:T(2,128)}), f32[128,2,2,512]{3,2,1,0:T(2,128)S(1)}, u32[]{:S(2)}, u32[]{:S(2)}) %all-to-all-start.9) | async-done | bytes 1048608 | tf_op jit(solution)/shard_map/all_to_all | solution.py:38
  326.9 8.0 %all-to-all-start.10 = ((f32[128,2,2,512]{3,2,1,0:T(2,128)}), f32[128,2,2,512]{3,2,1,0:T(2,128)S(1)}, u32[]{:S(2)}, u32[]{:S(2)}) async-start(f32[128,2,2,512]{3,2,1,0:T(2,128)} %copy.128), calls=%async_computation.11 | async-start | bytes 2097152 | tf_op jit(solution)/shard_map/all_to_all | solution.py:39
  341.4 17.4 %all-to-all-done.10 = f32[128,2,2,512]{3,2,1,0:T(2,128)S(1)} async-done(((f32[128,2,2,512]{3,2,1,0:T(2,128)}), f32[128,2,2,512]{3,2,1,0:T(2,128)S(1)}, u32[]{:S(2)}, u32[]{:S(2)}) %all-to-all-start.10) | async-done | bytes 1048608 | tf_op jit(solution)/shard_map/all_to_all | solution.py:39
  358.8 8.3 %all-to-all-start.5 = ((f32[128,2,2,256]{3,2,1,0:T(2,128)}), f32[128,2,2,256]{3,2,1,0:T(2,128)S(1)}, u32[]{:S(2)}, u32[]{:S(2)}) async-start(f32[128,2,2,256]{3,2,1,0:T(2,128)} %copy.105), calls=%async_computation.5 | async-start | bytes 1048576 | tf_op jit(solution)/shard_map/all_to_all | solution.py:32
  374.5 7.1 all-to-all-done.5
  381.6 7.3 all-to-all-start.11
  389.3 22.5 %all-to-all-done.11 = f32[128,2,2,512]{3,2,1,0:T(2,128)S(1)} async-done(((f32[128,2,2,512]{3,2,1,0:T(2,128)}), f32[128,2,2,512]{3,2,1,0:T(2,128)S(1)}, u32[]{:S(2)}, u32[]{:S(2)}) %all-to-all-start.11) | async-done | bytes 1048608 | tf_op jit(solution)/shard_map/all_to_all | solution.py:32
  417.0 344.0 %psum.14 = f32[256]{0:T(256)S(1)} all-reduce(f32[256]{0:T(256)S(1)} %copy-done.23), channel_id=1, replica_groups=mesh['ctx'=128,'ch'=2] {'ctx'}, use_global_device_ids=true, to_apply=%region_2.3 | all-reduce | flops 256 | bytes 2048 | tf_op jit(solution)/shard_map/psum | solution.py:171
  (152 shorter events, 128.9 us)
Async XLA Ops:
  13.7 15.6 %copy-start.17 = (f32[256,256]{1,0:T(8,128)S(1)}, f32[256,256]{1,0:T(8,128)}, u32[]{:S(2)}) copy-start(f32[256,256]{1,0:T(8,128)} %param.10) | copy-start | bytes 786436
  13.7 34.6 %all-to-all-start.6 = ((f32[128,2,2,256]{3,1,2,0:T(2,128)}), f32[128,2,2,256]{3,1,2,0:T(2,128)S(1)}, u32[]{:S(2)}, u32[]{:S(2)}) async-start(f32[128,2,2,256]{3,1,2,0:T(2,128)} %stack.7), calls=%async_computation.7 | async-start | bytes 1048576 | tf_op jit(solution)/shard_map/all_to_all | solution.py:32
  48.4 36.0 %all-to-all-start = ((f32[128,2,2,512]{3,1,2,0:T(2,128)}), f32[128,2,2,512]{3,1,2,0:T(2,128)S(1)}, u32[]{:S(2)}, u32[]{:S(2)}) async-start(f32[128,2,2,512]{3,1,2,0:T(2,128)} %stack.6.clone), calls=%async_computation | async-start | bytes 2097152 | tf_op jit(solution)/shard_map/all_to_all | solution.py:32
  84.4 25.3 %all-to-all-start.7 = ((f32[128,2,2,256]{3,2,1,0:T(2,128)}), f32[128,2,2,256]{3,2,1,0:T(2,128)S(1)}, u32[]{:S(2)}, u32[]{:S(2)}) async-start(f32[128,2,2,256]{3,2,1,0:T(2,128)} %bitcast.49), calls=%async_computation.8 | async-start | bytes 1048576 | tf_op jit(solution)/shard_map/all_to_all | solution.py:38
  109.6 23.9 %all-to-all-start.8 = ((f32[128,2,2,256]{3,2,1,0:T(2,128)}), f32[128,2,2,256]{3,2,1,0:T(2,128)S(1)}, u32[]{:S(2)}, u32[]{:S(2)}) async-start(f32[128,2,2,256]{3,2,1,0:T(2,128)} %bitcast.50), calls=%async_computation.9 | async-start | bytes 1048576 | tf_op jit(solution)/shard_map/all_to_all | solution.py:39
  133.5 9.3 %copy-start.1 = (f32[256,2,512]{2,0,1:T(8,128)S(1)}, f32[256,2,512]{2,0,1:T(8,128)}, u32[]{:S(2)}) copy-start(f32[256,2,512]{2,0,1:T(8,128)} %get-tuple-element.17) | copy-start | bytes 3145732
  133.5 33.6 %all-to-all-start.1 = ((f32[128,2,2,512]{3,2,1,0:T(2,128)}), f32[128,2,2,512]{3,2,1,0:T(2,128)S(1)}, u32[]{:S(2)}, u32[]{:S(2)}) async-start(f32[128,2,2,512]{3,2,1,0:T(2,128)} %bitcast.209), calls=%async_computation.1 | async-start | bytes 2097152 | tf_op jit(solution)/shard_map/all_to_all | solution.py:38
  167.1 33.1 %all-to-all-start.2 = ((f32[128,2,2,512]{3,2,1,0:T(2,128)}), f32[128,2,2,512]{3,2,1,0:T(2,128)S(1)}, u32[]{:S(2)}, u32[]{:S(2)}) async-start(f32[128,2,2,512]{3,2,1,0:T(2,128)} %bitcast.208), calls=%async_computation.2 | async-start | bytes 2097152 | tf_op jit(solution)/shard_map/all_to_all | solution.py:39
  237.8 23.2 %all-to-all-start.3 = ((f32[128,2,2,256]{3,2,1,0:T(2,128)}), f32[128,2,2,256]{3,2,1,0:T(2,128)S(1)}, u32[]{:S(2)}, u32[]{:S(2)}) async-start(f32[128,2,2,256]{3,2,1,0:T(2,128)} %copy.98), calls=%async_computation.3 | async-start | bytes 1048576 | tf_op jit(solution)/shard_map/all_to_all | solution.py:38
  248.7 4.6 copy-start.28
  261.8 27.1 %all-to-all-start.4 = ((f32[128,2,2,256]{3,2,1,0:T(2,128)}), f32[128,2,2,256]{3,2,1,0:T(2,128)}, u32[]{:S(2)}, u32[]{:S(2)}) async-start(f32[128,2,2,256]{3,2,1,0:T(2,128)} %copy.102), calls=%async_computation.4 | async-start | bytes 1048576 | tf_op jit(solution)/shard_map/all_to_all | solution.py:39
  274.2 4.6 copy-start.19
  274.2 4.6 copy-start.21
  274.2 4.6 copy-start.26
  274.2 4.6 copy-start.30
  274.3 4.6 copy-start.32
  288.9 37.9 %all-to-all-start.9 = ((f32[128,2,2,512]{3,2,1,0:T(2,128)}), f32[128,2,2,512]{3,2,1,0:T(2,128)S(1)}, u32[]{:S(2)}, u32[]{:S(2)}) async-start(f32[128,2,2,512]{3,2,1,0:T(2,128)} %copy.124), calls=%async_computation.10 | async-start | bytes 2097152 | tf_op jit(solution)/shard_map/all_to_all | solution.py:38
  326.9 8.1 %copy-start.22 = (f32[256,2]{0,1:T(2,128)S(1)}, f32[256,2]{0,1:T(2,128)}, u32[]{:S(2)}) copy-start(f32[256,2]{0,1:T(2,128)} %get-tuple-element.39) | copy-start | bytes 6148
  326.9 8.3 %copy-start.7 = (f32[128,2,2,256]{3,2,1,0:T(2,128)S(1)}, f32[128,2,2,256]{3,2,1,0:T(2,128)}, u32[]{:S(2)}) copy-start(f32[128,2,2,256]{3,2,1,0:T(2,128)} %copy-done.6) | copy-start | bytes 1572868
  326.9 31.9 %all-to-all-start.10 = ((f32[128,2,2,512]{3,2,1,0:T(2,128)}), f32[128,2,2,512]{3,2,1,0:T(2,128)S(1)}, u32[]{:S(2)}, u32[]{:S(2)}) async-start(f32[128,2,2,512]{3,2,1,0:T(2,128)} %copy.128), calls=%async_computation.11 | async-start | bytes 2097152 | tf_op jit(solution)/shard_map/all_to_all | solution.py:39
  358.8 22.8 %all-to-all-start.5 = ((f32[128,2,2,256]{3,2,1,0:T(2,128)}), f32[128,2,2,256]{3,2,1,0:T(2,128)S(1)}, u32[]{:S(2)}, u32[]{:S(2)}) async-start(f32[128,2,2,256]{3,2,1,0:T(2,128)} %copy.105), calls=%async_computation.5 | async-start | bytes 1048576 | tf_op jit(solution)/shard_map/all_to_all | solution.py:32
  381.6 30.2 %all-to-all-start.11 = ((f32[128,2,2,512]{3,2,1,0:T(2,128)}), f32[128,2,2,512]{3,2,1,0:T(2,128)S(1)}, u32[]{:S(2)}, u32[]{:S(2)}) async-start(f32[128,2,2,512]{3,2,1,0:T(2,128)} %copy.131), calls=%async_computation.12 | async-start | bytes 2097152 | tf_op jit(solution)/shard_map/all_to_all | solution.py:32
  388.9 372.6 %all-reduce.4.cloned.1.call-start = ((), (), s32[]{:S(2)}) async-start(), calls=%async_computation.14 | async-start | bytes 1048576 | tf_op jit(solution)/shard_map/psum | solution.py:171
  415.2 348.2 %reduce-scatter.2.cloned.1.call-start = ((), (), s32[]{:S(2)}) async-start(), calls=%async_computation.13 | async-start | bytes 786432 | tf_op jit(solution)/shard_map/reduce_scatter | solution.py:144
  (23 other events, 45.3 us)
Sparse Core Ops, SparseCore 0:
  415.3 211.7 all-reduce.3
Sparse Core Ops, SparseCore 1:
  418.1 8.6 reduce-scatter.1
where the time goes:
time: 782 us; the launch traced here: 773 us
  blocking collectives  346 us (44%)
  waiting for transfers between devices  167 us (21%)
  starting transfers between devices  113 us (14%)
  matrix products  96.9 us (12%)
  local copies, waits for them, and re-layouts  23.5 us (3%)
  between operations  16.8 us (2%)
  other arithmetic  9.23 us (1%)
    psum x1, blocking collectives, shards(): weight_sum, skip_sum = lax.psum((weight_part, skip_part), 'ctx')  344 us
    all_to_all x4, waiting for transfers between devices, route_signal(): lax.all_to_all(blocks, 'ctx', split_axis=0, concat_axis=0, tiled=True)  69.6 us
    all_to_all x4, waiting for transfers between devices, route_spectrum(): lax.all_to_all(spec_re, 'ctx', split_axis=0, concat_axis=0, tiled=True)  59.7 us
    all_to_all x4, starting transfers between devices, route_signal(): lax.all_to_all(blocks, 'ctx', split_axis=0, concat_axis=0, tiled=True)  38.7 us
    all_to_all x4, waiting for transfers between devices, route_spectrum(): lax.all_to_all(spec_im, 'ctx', split_axis=0, concat_axis=0, tiled=True)  38 us
    all_to_all x4, starting transfers between devices, route_spectrum(): lax.all_to_all(spec_re, 'ctx', split_axis=0, concat_axis=0, tiled=True)  37.7 us
    all_to_all x4, starting transfers between devices, route_spectrum(): lax.all_to_all(spec_im, 'ctx', split_axis=0, concat_axis=0, tiled=True)  36.2 us
    dot_general x8, matrix products, apply_table(): exact_einsum(form, wave_im, sig_im)  21.5 us
  transfers between devices with their start and end apart: 14, of which 11 were waited for; matrix products, arithmetic and copies ran while one was open for 11% of the time, Pallas kernels for 0%

commit v1 on v0

v1 whole, which is shorter than its diff:
```python
import math

import jax
import jax.numpy as jnp
import numpy as np
import ml_dtypes
from jax import lax
from jax.experimental import pallas as pl
from jax.experimental.pallas import tpu as pltpu
from jax.sharding import PartitionSpec as P

MESH = pl.DeviceIdType.MESH
F32, BF16 = jnp.float32, jnp.bfloat16
NCTX = 128
NY, NZ, NX = 4, 8, 4
LEN = 32768
ROOT = math.sqrt(LEN)


def split_table(table):
    table = table.astype(np.float32)
    hi = table.astype(ml_dtypes.bfloat16)
    lo = (table - hi.astype(np.float32)).astype(ml_dtypes.bfloat16)
    return hi, lo


def tables():
    n1 = np.arange(128)
    n2 = np.arange(256)
    ang = -2 * np.pi * ((n1[None, :] * (4 * n1[:, None] + 1)) % 512) / 512
    a_hi, a_lo = split_table(np.concatenate([np.cos(ang), np.sin(ang)], 0))
    a_cat = np.concatenate([a_hi, a_lo], 1)
    c_hi, c_lo = split_table(np.concatenate([np.cos(ang.T), np.sin(ang.T)], 1) / LEN)
    c_cat = np.concatenate([c_hi, c_lo, c_hi], 1)
    tw = -2 * np.pi * ((n2[None, :] * (4 * n1[:, None] + 1)) % (4 * LEN)) / (4 * LEN)
    t_re, t_im = np.cos(tw).astype(np.float32), np.sin(tw).astype(np.float32)
    bang = -2 * np.pi * ((n2[:, None] * n2[None, :]) % 256) / 256
    b_hi, b_lo = split_table(np.concatenate([np.cos(bang), np.sin(bang)], 1))
    b_cat = np.concatenate([b_hi, b_lo, b_hi], 0)
    return a_cat, b_cat, c_cat, t_re, t_im


def dot(a, b, dims=(((1,), (0,)), ((), ()))):
    return lax.dot_general(a, b, dims, preferred_element_type=F32)


def split(val):
    hi = val.astype(BF16)
    return hi, (val - hi.astype(F32)).astype(BF16)


def kernel(
    q_ref, k_ref, v_ref, taps_ref, skip_ref, w_ref, g_ref, a_ref, b_ref, c_ref, tr_ref, ti_ref,
    out_ref, gq_ref, gk_ref, gv_ref, gf_ref, gs_ref, gw_ref,
    s1, r1, s2, r2, s3, r3, s4, r4,
    i8, i4, prod, dmix, dgat, gfull, gboth, w_oth, gat_oth,
    sig_re, sig_im, tap_re, tap_im,
    g1, rg, sz, rz, az, ga, sk, rsk1, sk2, rsk2,
    lsem, ssem, rsem,
):
    me = lax.axis_index("ctx")
    ch = lax.axis_index("ch")
    y, z, x = me // 32, lax.rem(me // 4, NZ), lax.rem(me, NX)
    plane = y * NX + x

    def peer(idx):
        return {"ctx": idx}

    def remote(src, dst, sem, device):
        return pltpu.make_async_remote_copy(
            src_ref=src, dst_ref=dst, send_sem=ssem.at[sem], recv_sem=rsem.at[sem],
            device_id=device, device_id_type=MESH,
        )

    def at_plane(idx):
        return peer(idx // NX * 32 + z * NX + lax.rem(idx, NX))

    def at_z(idx):
        return peer(y * 32 + idx * NX + x)

    sibling = {"ch": 1 - ch}

    bar = pltpu.get_barrier_semaphore()

    def greet(step, carry):
        pl.semaphore_signal(bar, inc=1, device_id=peer(lax.rem(me + step, NCTX)), device_id_type=MESH)
        return carry

    lax.fori_loop(1, NCTX, greet, 0)
    pl.semaphore_signal(bar, inc=1, device_id=sibling, device_id_type=MESH)

    def interleave(blocks, tmp, dst):
        rows = len(blocks)
        for r, blk in enumerate(blocks):
            tmp[pl.ds(r, 128, stride=rows), :] = blk
        dst[...] = tmp[...].reshape(128, rows, 128).astype(BF16)

    def separate(src, tmp, rows):
        tmp[...] = src[...].astype(F32).reshape(128 * rows, 128)
        return [tmp[pl.ds(r, 128, stride=rows), :] for r in range(rows)]

    def send_all(src, dst, sem, lslot):
        pltpu.make_async_copy(src.at[me], dst.at[me], lsem.at[lslot]).start()

        def go(step, carry):
            to = lax.rem(me + step, NCTX)
            remote(src.at[to], dst.at[me], sem, peer(to)).start()
            return carry

        lax.fori_loop(1, NCTX, go, 0)

    def wait_all(src, dst, sem, lslot):
        pltpu.make_async_copy(src.at[me], dst.at[me], lsem.at[lslot]).wait()
        whole = remote(
            src.at[pl.ds(0, NCTX - 1)], dst.at[pl.ds(0, NCTX - 1)], sem, peer(lax.rem(me + 1, NCTX))
        )
        whole.wait_recv()
        whole.wait_send()

    def blocks_of(val):
        return [
            val[th * 128:(th + 1) * 128, h * 128:(h + 1) * 128].T for h in range(2) for th in range(2)
        ]

    def tokens_of(blks):
        return jnp.concatenate(
            [jnp.concatenate([blks[th].T, blks[2 + th].T], 1) for th in range(2)], 0
        )

    def forward(blks):
        sig = jnp.concatenate(blks, 1).astype(BF16)
        spec = dot(a_ref[...], jnp.concatenate([sig, sig], 0))
        re, im = spec[:128], spec[128:]
        t_re, t_im = tr_ref[...], ti_ref[...]
        top, bottom = [], []
        for h in range(2):
            u, w = re[:, h * 256:(h + 1) * 256], im[:, h * 256:(h + 1) * 256]
            top.append(u * t_re - w * t_im)
            bottom.append(u * t_im + w * t_re)
        hi, lo = split(jnp.concatenate(top + bottom, 0))
        full = dot(jnp.concatenate([hi, hi, lo], 1), b_ref[...])
        return full[:256, :256] - full[256:, 256:], full[:256, 256:] + full[256:, :256]

    def inverse(re, im):
        hi, lo = split(jnp.concatenate([re, im], 0))
        full = dot(jnp.concatenate([hi, hi, lo], 1), b_ref[...])
        u = full[:256, :256] + full[256:, 256:]
        w = full[256:, :256] - full[:256, 256:]
        t_re, t_im = tr_ref[...], ti_ref[...]
        top, bottom = [], []
        for h in range(2):
            ur, wi = u[h * 128:(h + 1) * 128], w[h * 128:(h + 1) * 128]
            top.append(ur * t_re + wi * t_im)
            bottom.append(wi * t_re - ur * t_im)
        both = jnp.concatenate([jnp.concatenate(top, 1), jnp.concatenate(bottom, 1)], 0)
        hi, lo = split(both)
        sig = dot(c_ref[...], jnp.concatenate([hi, hi, lo], 0))
        return [sig[:, r * 128:(r + 1) * 128] for r in range(4)]

    prod[...] = k_ref[...].astype(F32) * v_ref[...].astype(F32)
    interleave(blocks_of(prod[...]) + blocks_of(taps_ref[...]), i8, s1)
    pl.semaphore_wait(bar, NCTX)
    g_send = remote(g_ref, gboth, 8, sibling)
    g_send.start()
    w_send = remote(w_ref.at[:, pl.ds(pl.multiple_of((1 - ch) * 256, 256), 256)], w_oth, 9, sibling)
    w_send.start()
    send_all(s1, r1, 0, 0)

    g_send.wait()
    mine, other = g_ref[...], gboth[...]
    first = ch == 0
    gfull[:, :256] = jnp.where(first, mine.astype(F32), other.astype(F32)).astype(BF16)
    gfull[:, 256:] = jnp.where(first, other.astype(F32), mine.astype(F32)).astype(BF16)
    dgat[...] = dot(gfull[...], w_ref[...], (((1,), (1,)), ((), ())))
    dmix[...] = dgat[...] * q_ref[...].astype(F32)
    interleave(blocks_of(dmix[...]), i4, s2)
    send_all(s2, r2, 1, 1)

    sk[...] = jnp.broadcast_to(jnp.sum(dmix[...] * prod[...], axis=0, keepdims=True), (8, 256))
    for step in range(1, 16):
        remote(sk, rsk1.at[plane], 4, at_plane(lax.rem(plane + step, 16))).start()

    wait_all(s1, r1, 0, 0)
    blks = separate(r1, i8, 8)
    re, im = forward(blks[:4])
    sig_re[...], sig_im[...] = re, im
    re, im = forward(blks[4:])
    tap_re[...], tap_im[...] = re, im
    re, im = sig_re[...], sig_im[...]
    conv = inverse(re * tap_re[...] - im * tap_im[...], re * tap_im[...] + im * tap_re[...])
    interleave(conv, i4, s3)
    send_all(s3, r3, 2, 2)

    wsk = remote(rsk1.at[pl.ds(0, 15)], rsk1.at[pl.ds(0, 15)], 4, at_plane(lax.rem(plane + 1, 16)))
    wsk.wait_recv()
    wsk.wait_send()
    rsk1[plane] = sk[...]
    sk2[...] = jnp.sum(rsk1[...], axis=0)
    for step in range(1, NZ):
        remote(sk2, rsk2.at[z], 5, at_z(lax.rem(z + step, NZ))).start()

    wait_all(s2, r2, 1, 1)
    re, im = forward(separate(r2, i4, 4))
    lag_p = inverse(re * tap_re[...] + im * tap_im[...], im * tap_re[...] - re * tap_im[...])
    lag_f = inverse(re * sig_re[...] + im * sig_im[...], im * sig_re[...] - re * sig_im[...])
    interleave(lag_p + lag_f, i8, s4)
    send_all(s4, r4, 3, 3)

    wait_all(s3, r3, 2, 2)
    skip = skip_ref[...]
    mixed = tokens_of(separate(r3, i4, 4)) + skip * prod[...]
    gated = (q_ref[...].astype(F32) * mixed).astype(BF16)
    gq_ref[...] = (dgat[...] * mixed).astype(BF16)
    g1[...] = dot(gated, gfull[...], (((0,), (0,)), ((), ()))).astype(BF16)
    for step in range(1, 16):
        to = lax.rem(plane + step, 16)
        remote(
            g1.at[pl.ds(pl.multiple_of(to * 16, 16), 16)], rg.at[plane], 6, at_plane(to)
        ).start()
    s_gat = gat_oth.at[0]
    gat_oth[0] = gated
    gat_send = remote(s_gat, gat_oth.at[1], 10, sibling)
    gat_send.start()
    w_send.wait()
    w_mine = w_ref[:, pl.ds(pl.multiple_of(ch * 256, 256), 256)]
    part = dot(gated, w_mine)
    gat_send.wait()
    out_ref[...] = (part + dot(gat_oth[1], w_oth[...])).astype(BF16)

    wrg = remote(rg.at[pl.ds(0, 15)], rg.at[pl.ds(0, 15)], 6, at_plane(lax.rem(plane + 1, 16)))
    wrg.wait_recv()
    wrg.wait_send()
    rg[plane] = g1[pl.ds(pl.multiple_of(plane * 16, 16), 16), :]
    total = jnp.sum(rg[...].astype(F32), axis=0)
    for i in range(NZ):
        sz[i] = total[i // 4 * 8:i // 4 * 8 + 8, i % 4 * 128:i % 4 * 128 + 128]
    for step in range(1, NZ):
        to = lax.rem(z + step, NZ)
        remote(sz.at[to], rz.at[z], 7, at_z(to)).start()
    wsk = remote(rsk2.at[pl.ds(0, 7)], rsk2.at[pl.ds(0, 7)], 5, at_z(lax.rem(z + 1, NZ)))
    wsk.wait_recv()
    wsk.wait_send()
    rsk2[z] = sk2[...]
    gs_ref[...] = jnp.sum(rsk2[...], axis=0) / ROOT
    wrz = remote(rz.at[pl.ds(0, 7)], rz.at[pl.ds(0, 7)], 7, at_z(lax.rem(z + 1, NZ)))
    wrz.wait_recv()
    wrz.wait_send()
    rz[z] = sz[z]
    az[z] = jnp.sum(rz[...], axis=0) / ROOT
    for step in range(1, NZ):
        remote(az.at[z], az.at[z], 11, at_z(lax.rem(z + step, NZ))).start()
    waz = remote(az.at[pl.ds(0, 7)], az.at[pl.ds(0, 7)], 11, at_z(lax.rem(z + 1, NZ)))
    waz.wait_recv()
    waz.wait_send()
    rows = [jnp.concatenate([az[4 * i + j] for j in range(4)], 1) for i in range(2)]
    ga[plane] = jnp.concatenate(rows, 0).astype(BF16)
    for step in range(1, 16):
        remote(ga.at[plane], ga.at[plane], 12, at_plane(lax.rem(plane + step, 16))).start()

    wait_all(s4, r4, 3, 3)
    blks = separate(r4, i8, 8)
    grad_prod = tokens_of(blks[:4]) + skip * dmix[...]
    gk_ref[...] = (grad_prod * v_ref[...].astype(F32)).astype(BF16)
    gv_ref[...] = (grad_prod * k_ref[...].astype(F32)).astype(BF16)
    gf_ref[...] = tokens_of(blks[4:]) / ROOT

    wga = remote(ga.at[pl.ds(0, 15)], ga.at[pl.ds(0, 15)], 12, at_plane(lax.rem(plane + 1, 16)))
    wga.wait_recv()
    wga.wait_send()
    gw_ref[...] = ga[...].astype(F32).reshape(256, 512)


def shards(query_act, key_act, value_act, filter_taps, skip_gain, out_weight, out_grad):
    a_cat, b_cat, c_cat, t_re, t_im = (jnp.asarray(t) for t in tables())
    vmem = pl.BlockSpec(memory_space=pltpu.VMEM)
    sds = jax.ShapeDtypeStruct
    outs = pl.pallas_call(
        kernel,
        out_shape=(
            sds((256, 256), BF16), sds((256, 256), BF16), sds((256, 256), BF16),
            sds((256, 256), BF16), sds((256, 256), F32), sds((8, 256), F32), sds((256, 512), F32),
        ),
        in_specs=[vmem] * 12,
        out_specs=[vmem] * 7,
        scratch_shapes=[
            pltpu.VMEM((128, 8, 128), BF16), pltpu.VMEM((128, 8, 128), BF16),
            pltpu.VMEM((128, 4, 128), BF16), pltpu.VMEM((128, 4, 128), BF16),
            pltpu.VMEM((128, 4, 128), BF16), pltpu.VMEM((128, 4, 128), BF16),
            pltpu.VMEM((128, 8, 128), BF16), pltpu.VMEM((128, 8, 128), BF16),
            pltpu.VMEM((1024, 128), F32), pltpu.VMEM((512, 128), F32),
            pltpu.VMEM((256, 256), F32), pltpu.VMEM((256, 256), F32), pltpu.VMEM((256, 256), F32),
            pltpu.VMEM((256, 512), BF16), pltpu.VMEM((256, 256), BF16),
            pltpu.VMEM((256, 256), BF16), pltpu.VMEM((2, 256, 256), BF16),
            pltpu.VMEM((256, 256), F32), pltpu.VMEM((256, 256), F32),
            pltpu.VMEM((256, 256), F32), pltpu.VMEM((256, 256), F32),
            pltpu.VMEM((256, 512), BF16), pltpu.VMEM((16, 16, 512), BF16),
            pltpu.VMEM((8, 8, 128), F32), pltpu.VMEM((8, 8, 128), F32), pltpu.VMEM((8, 8, 128), F32),
            pltpu.VMEM((16, 16, 512), BF16),
            pltpu.VMEM((8, 256), F32), pltpu.VMEM((16, 8, 256), F32),
            pltpu.VMEM((8, 256), F32), pltpu.VMEM((8, 8, 256), F32),
            pltpu.SemaphoreType.DMA((4,)), pltpu.SemaphoreType.DMA((13,)), pltpu.SemaphoreType.DMA((13,)),
        ],
        compiler_params=pltpu.CompilerParams(
            collective_id=0, has_side_effects=True, vmem_limit_bytes=48 * 1024 * 1024
        ),
        name="hyena",
    )(
        query_act, key_act, value_act, filter_taps, skip_gain[None, :], out_weight, out_grad,
        a_cat, b_cat, c_cat, t_re, t_im,
    )
    out, gq, gk, gv, gf, gs, gw = outs
    return out, gq, gk, gv, gf, gs[0], gw


def solution(mesh):
    spec = P("ctx", "ch")
    in_specs = (spec, spec, spec, spec, P("ch"), P("ch", None), spec)
    out_specs = (spec, spec, spec, spec, spec, P("ch"), P("ch", None))
    return jax.shard_map(shards, mesh=mesh, in_specs=in_specs, out_specs=out_specs, check_vma=False)
```

time: 782 us -> 72 us (0.09); the launches traced: 773 us -> 71.2 us
  blocking collectives: 346 us -> 0 us
  waiting for transfers between devices: 167 us -> 0 us
  starting transfers between devices: 113 us -> 0 us
  matrix products: 96.9 us -> 0 us
  Pallas kernels: 0 us -> 54.9 us
  between operations: 16.8 us -> 0.67 us
  other arithmetic: 9.23 us -> 0 us
  local copies, waits for them, and re-layouts: 23.5 us -> 15.6 us
    psum x1 -> x0, blocking collectives: 344 us -> none  [shards(): weight_sum, skip_sum = lax.psum((weight_part, skip_part), 'ctx')]
    all_to_all x12 -> x0, waiting for transfers between devices: 167 us -> none  [the longest x4 69.6 us: route_signal(): lax.all_to_all(blocks, 'ctx', split_axis=0, concat_axis=0, tiled=True)]
    all_to_all x12 -> x0, starting transfers between devices: 113 us -> none  [the longest x4 38.7 us: route_signal(): lax.all_to_all(blocks, 'ctx', split_axis=0, concat_axis=0, tiled=True)]
    dot_general x43 -> x0, matrix products: 96.9 us -> none  [the longest x8 21.5 us: apply_table(): exact_einsum(form, wave_im, sig_im)]
    pallas_call x0 -> x1, Pallas kernels: none -> 54.9 us  [shards(): pl.pallas_call(kernel, out_shape=(sds((256, 256), BF16), sds((256, 256),...]
    unnamed x66 -> x30, local copies, waits for them, and re-layouts: 2.77 us -> 15.1 us
  transfers between devices with their start and end apart: 14 -> 0, of which waited for: 11 -> 0; matrix products, arithmetic and copies ran while one was open for 11% -> 0% of each run, Pallas kernels for 0% -> 0%
where the time goes in v1:
time: 72 us; the launch traced here: 71.2 us
  Pallas kernels  54.9 us (76%)
  local copies, waits for them, and re-layouts  15.6 us (22%)
    pallas_call x1, Pallas kernels, shards(): pl.pallas_call(kernel, out_shape=(sds((256, 256), BF16), sds((256, 256),...  54.9 us
    unnamed x30, local copies, waits for them, and re-layouts  15.1 us

profile of v1, /device:TPU:2, one launch (start us, length us, event | category | flops | bytes accessed | tf_op | source)
XLA Modules:
  0.0 71.2 jit_solution(7090836351745727140)
XLA Ops:
  0.6 0.0 copy-start.11
  0.6 0.7 copy-done.11
  1.3 0.0 copy-start
  1.3 1.1 %copy-done = bf16[768,512]{1,0:T(8,128)(2,1)S(1)} copy-done((bf16[768,512]{1,0:T(8,128)(2,1)S(1)}, bf16[768,512]{1,0:T(8,128)(2,1)}, u32[]{:S(2)}) %copy-start) | copy-done | bytes 786456
  2.4 0.0 copy-start.1
  2.5 0.9 %copy-done.1 = f32[256,256]{1,0:T(8,128)S(1)} copy-done((f32[256,256]{1,0:T(8,128)S(1)}, f32[256,256]{1,0:T(8,128)}, u32[]{:S(2)}) %copy-start.1) | copy-done | bytes 262168
  3.4 0.0 copy-start.2
  3.4 0.9 %copy-done.2 = bf16[256,512]{1,0:T(8,128)(2,1)S(1)} copy-done((bf16[256,512]{1,0:T(8,128)(2,1)S(1)}, bf16[256,512]{1,0:T(8,128)(2,1)}, u32[]{:S(2)}) %copy-start.2) | copy-done | bytes 262168
  4.4 0.9 %copy-done.3 = bf16[128,768]{1,0:T(8,128)(2,1)S(1)} copy-done((bf16[128,768]{1,0:T(8,128)(2,1)S(1)}, bf16[128,768]{1,0:T(8,128)(2,1)}, u32[]{:S(2)}) %copy-start.3) | copy-done | bytes 196632
  5.3 0.9 %copy-done.4 = bf16[256,256]{1,0:T(8,128)(2,1)S(1)} copy-done((bf16[256,256]{1,0:T(8,128)(2,1)S(1)}, bf16[256,256]{1,0:T(8,128)(2,1)}, u32[]{:S(2)}) %copy-start.4) | copy-done | bytes 131096
  6.2 0.9 %copy-done.5 = bf16[256,256]{1,0:T(8,128)(2,1)S(1)} copy-done((bf16[256,256]{1,0:T(8,128)(2,1)S(1)}, bf16[256,256]{1,0:T(8,128)(2,1)}, u32[]{:S(2)}) %copy-start.5) | copy-done | bytes 131096
  7.1 0.9 %copy-done.6 = bf16[256,256]{1,0:T(8,128)(2,1)S(1)} copy-done((bf16[256,256]{1,0:T(8,128)(2,1)S(1)}, bf16[256,256]{1,0:T(8,128)(2,1)}, u32[]{:S(2)}) %copy-start.6) | copy-done | bytes 131096
  8.0 0.9 %copy-done.7 = bf16[256,256]{1,0:T(8,128)(2,1)S(1)} copy-done((bf16[256,256]{1,0:T(8,128)(2,1)S(1)}, bf16[256,256]{1,0:T(8,128)(2,1)}, u32[]{:S(2)}) %copy-start.7) | copy-done | bytes 131096
  8.9 0.9 %copy-done.8 = f32[128,256]{1,0:T(8,128)S(1)} copy-done((f32[128,256]{1,0:T(8,128)S(1)}, f32[128,256]{1,0:T(8,128)}, u32[]{:S(2)}) %copy-start.8) | copy-done | bytes 131096
  9.8 0.9 %copy-done.9 = f32[128,256]{1,0:T(8,128)S(1)} copy-done((f32[128,256]{1,0:T(8,128)S(1)}, f32[128,256]{1,0:T(8,128)}, u32[]{:S(2)}) %copy-start.9) | copy-done | bytes 131096
  10.7 0.9 %copy-done.10 = bf16[256,256]{1,0:T(8,128)(2,1)S(1)} copy-done((bf16[256,256]{1,0:T(8,128)(2,1)S(1)}, bf16[256,256]{1,0:T(8,128)(2,1)}, u32[]{:S(2)}) %copy-start.10) | copy-done | bytes 131096
  11.6 54.9 %hyena.1 = (bf16[256,256]{1,0:T(8,128)(2,1)S(1)}, bf16[256,256]{1,0:T(8,128)(2,1)S(1)}, bf16[256,256]{1,0:T(8,128)(2,1)S(1)}, bf16[256,256]{1,0:T(8,128)(2,1)S(1...) custom-call(bf16[256,256]{1,0:T(8,128)(2,1)S(1)} %copy-done.4, ...), custom_call_target="tpu_custom_call" | custom-call | tf_op jit(solution)/shard_map/hyena/pallas_call | solution.py:277
  66.5 0.6 slice.3
  67.1 0.7 copy.25
  67.8 0.7 copy.26
  68.4 0.7 copy.27
  69.1 0.7 copy.28
  69.7 0.7 copy.29
  70.4 0.8 %copy.30 = f32[256,512]{1,0:T(8,128)} copy(f32[256,512]{1,0:T(8,128)S(1)} %get-tuple-element.34) | data formatting | bytes 1048576
  (8 shorter events, 0.0 us)
Async XLA Ops:
  0.6 0.7 copy-start.11
  1.3 1.1 %copy-start = (bf16[768,512]{1,0:T(8,128)(2,1)S(1)}, bf16[768,512]{1,0:T(8,128)(2,1)}, u32[]{:S(2)}) copy-start(bf16[768,512]{1,0:T(8,128)(2,1)} %constant.11.clone.b_ref) | copy-start | bytes 2359300
  2.4 0.9 %copy-start.1 = (f32[256,256]{1,0:T(8,128)S(1)}, f32[256,256]{1,0:T(8,128)}, u32[]{:S(2)}) copy-start(f32[256,256]{1,0:T(8,128)} %taps_ref.1) | copy-start | bytes 786436
  3.4 0.9 %copy-start.2 = (bf16[256,512]{1,0:T(8,128)(2,1)S(1)}, bf16[256,512]{1,0:T(8,128)(2,1)}, u32[]{:S(2)}) copy-start(bf16[256,512]{1,0:T(8,128)(2,1)} %w_ref.1) | copy-start | bytes 786436
  4.3 0.9 %copy-start.3 = (bf16[128,768]{1,0:T(8,128)(2,1)S(1)}, bf16[128,768]{1,0:T(8,128)(2,1)}, u32[]{:S(2)}) copy-start(bf16[128,768]{1,0:T(8,128)(2,1)} %constant.12.clone.c_ref) | copy-start | bytes 589828
  5.3 0.9 %copy-start.4 = (bf16[256,256]{1,0:T(8,128)(2,1)S(1)}, bf16[256,256]{1,0:T(8,128)(2,1)}, u32[]{:S(2)}) copy-start(bf16[256,256]{1,0:T(8,128)(2,1)} %q_ref.1) | copy-start | bytes 393220
  6.2 0.9 %copy-start.5 = (bf16[256,256]{1,0:T(8,128)(2,1)S(1)}, bf16[256,256]{1,0:T(8,128)(2,1)}, u32[]{:S(2)}) copy-start(bf16[256,256]{1,0:T(8,128)(2,1)} %k_ref.1) | copy-start | bytes 393220
  7.1 0.9 %copy-start.6 = (bf16[256,256]{1,0:T(8,128)(2,1)S(1)}, bf16[256,256]{1,0:T(8,128)(2,1)}, u32[]{:S(2)}) copy-start(bf16[256,256]{1,0:T(8,128)(2,1)} %v_ref.1) | copy-start | bytes 393220
  8.0 0.9 %copy-start.7 = (bf16[256,256]{1,0:T(8,128)(2,1)S(1)}, bf16[256,256]{1,0:T(8,128)(2,1)}, u32[]{:S(2)}) copy-start(bf16[256,256]{1,0:T(8,128)(2,1)} %g_ref.1) | copy-start | bytes 393220
  8.9 0.9 %copy-start.8 = (f32[128,256]{1,0:T(8,128)S(1)}, f32[128,256]{1,0:T(8,128)}, u32[]{:S(2)}) copy-start(f32[128,256]{1,0:T(8,128)} %constant.14.clone.ti_ref) | copy-start | bytes 393220
  9.8 0.9 %copy-start.9 = (f32[128,256]{1,0:T(8,128)S(1)}, f32[128,256]{1,0:T(8,128)}, u32[]{:S(2)}) copy-start(f32[128,256]{1,0:T(8,128)} %constant.13.clone.tr_ref) | copy-start | bytes 393220
  10.7 0.9 %copy-start.10 = (bf16[256,256]{1,0:T(8,128)(2,1)S(1)}, bf16[256,256]{1,0:T(8,128)(2,1)}, u32[]{:S(2)}) copy-start(bf16[256,256]{1,0:T(8,128)(2,1)} %constant.10.clone.a_ref) | copy-start | bytes 393220

commit v2 on v1

v2 whole, which is shorter than its diff:
```python
import math

import jax
import jax.numpy as jnp
import numpy as np
import ml_dtypes
from jax import lax
from jax.experimental import pallas as pl
from jax.experimental.pallas import tpu as pltpu
from jax.sharding import PartitionSpec as P

MESH = pl.DeviceIdType.MESH
F32, BF16 = jnp.float32, jnp.bfloat16
NCTX = 128
NY, NZ, NX = 4, 8, 4
LEN = 32768
ROOT = math.sqrt(LEN)


def split_table(table):
    table = table.astype(np.float32)
    hi = table.astype(ml_dtypes.bfloat16)
    lo = (table - hi.astype(np.float32)).astype(ml_dtypes.bfloat16)
    return hi, lo


def tables():
    n1 = np.arange(128)
    n2 = np.arange(256)
    ang = -2 * np.pi * ((n1[None, :] * (4 * n1[:, None] + 1)) % 512) / 512
    a_hi, a_lo = split_table(np.concatenate([np.cos(ang), np.sin(ang)], 0))
    a_cat = np.concatenate([a_hi, a_lo], 1)
    c_hi, c_lo = split_table(np.concatenate([np.cos(ang.T), np.sin(ang.T)], 1) / LEN)
    c_cat = np.concatenate([c_hi, c_lo, c_hi], 1)
    tw = -2 * np.pi * ((n2[None, :] * (4 * n1[:, None] + 1)) % (4 * LEN)) / (4 * LEN)
    t_re, t_im = np.cos(tw).astype(np.float32), np.sin(tw).astype(np.float32)
    bang = -2 * np.pi * ((n2[:, None] * n2[None, :]) % 256) / 256
    b_hi, b_lo = split_table(np.concatenate([np.cos(bang), np.sin(bang)], 1))
    b_cat = np.concatenate([b_hi, b_lo, b_hi], 0)
    return a_cat, b_cat, c_cat, t_re, t_im


def dot(a, b, dims=(((1,), (0,)), ((), ()))):
    return lax.dot_general(a, b, dims, preferred_element_type=F32)


def split(val):
    hi = val.astype(BF16)
    return hi, (val - hi.astype(F32)).astype(BF16)


ORDER4 = (2, 1, 3, 0)
ORDER8 = (4, 3, 5, 2, 6, 1, 7, 0)


def kernel(
    q_hbm, k_hbm, v_hbm, taps_hbm, skip_hbm, w_hbm, g_hbm, a_hbm, b_hbm, c_hbm, tr_hbm, ti_hbm,
    out_ref, gq_ref, gk_ref, gv_ref, gf_ref, gs_ref, gw_ref,
    q_ref, k_ref, v_ref, taps_ref, skip_ref, w_ref, g_ref, a_ref, b_ref, c_ref, tr_ref, ti_ref,
    s0, r0, s1, r1, s2, r2, s3, r3, s4, r4,
    i8, i4, prod, dmix, dgat, gfull, gboth, w_oth, gat_oth,
    sig_re, sig_im, tap_re, tap_im,
    g1, rg, sz, rz, az, ga, sk, rsk1, sk2, rsk2,
    isem, lsem, ssem, rsem,
):
    me = lax.axis_index("ctx")
    ch = lax.axis_index("ch")
    y, z, x = me // 32, lax.rem(me // 4, NZ), lax.rem(me, NX)
    plane = y * NX + x

    loads = {}
    pairs = (
        (k_hbm, k_ref), (v_hbm, v_ref), (taps_hbm, taps_ref), (g_hbm, g_ref), (w_hbm, w_ref),
        (q_hbm, q_ref), (a_hbm, a_ref), (tr_hbm, tr_ref), (ti_hbm, ti_ref), (b_hbm, b_ref),
        (c_hbm, c_ref), (skip_hbm, skip_ref),
    )
    for i, (src, dst) in enumerate(pairs):
        loads[i] = pltpu.make_async_copy(src, dst, isem.at[i])
        loads[i].start()

    def peer(idx):
        return {"ctx": idx}

    def remote(src, dst, sem, device):
        return pltpu.make_async_remote_copy(
            src_ref=src, dst_ref=dst, send_sem=ssem.at[sem], recv_sem=rsem.at[sem],
            device_id=device, device_id_type=MESH,
        )

    def at_plane(idx):
        return peer(idx // NX * 32 + z * NX + lax.rem(idx, NX))

    def at_z(idx):
        return peer(y * 32 + idx * NX + x)

    plane_order = [
        lax.rem(y + dy, NY) * NX + lax.rem(x + dx, NX) for dy in ORDER4 for dx in ORDER4
    ][:15]
    z_order = [lax.rem(z + dz, NZ) for dz in ORDER8][:7]
    sibling = {"ch": 1 - ch}

    bar = pltpu.get_barrier_semaphore()

    def greet(step, carry):
        pl.semaphore_signal(bar, inc=1, device_id=peer(lax.rem(me + 1 + step, NCTX)), device_id_type=MESH)
        return carry

    lax.fori_loop(0, NCTX - 1, greet, 0)
    pl.semaphore_signal(bar, inc=1, device_id=sibling, device_id_type=MESH)

    def interleave(blocks, tmp, dst):
        rows = len(blocks)
        for r, blk in enumerate(blocks):
            tmp[pl.ds(r, 128, stride=rows), :] = blk
        dst[...] = tmp[...].reshape(128, rows, 128).astype(BF16)

    def separate(src, tmp, rows):
        tmp[...] = src[...].astype(F32).reshape(128 * rows, 128)
        return [tmp[pl.ds(r, 128, stride=rows), :] for r in range(rows)]

    def send_all(src, dst, sem):
        pltpu.make_async_copy(src.at[me], dst.at[me], lsem.at[sem]).start()

        def go(step, carry):
            to = lax.rem(me + 1 + step, NCTX)
            remote(src.at[to], dst.at[me], sem, peer(to)).start()
            return carry

        lax.fori_loop(0, NCTX - 1, go, 0)

    def whole(src, dst, sem):
        return remote(
            src.at[pl.ds(0, NCTX - 1)], dst.at[pl.ds(0, NCTX - 1)], sem, peer(lax.rem(me + 1, NCTX))
        )

    def wait_all(src, dst, sem):
        pltpu.make_async_copy(src.at[me], dst.at[me], lsem.at[sem]).wait()
        whole(src, dst, sem).wait_recv()

    def some(buf, count, sem, device):
        part = buf.at[pl.ds(0, count)]
        return remote(part, part, sem, device)

    def blocks_of(val):
        return [
            val[th * 128:(th + 1) * 128, h * 128:(h + 1) * 128].T for h in range(2) for th in range(2)
        ]

    def tokens_of(blks):
        return jnp.concatenate(
            [jnp.concatenate([blks[th].T, blks[2 + th].T], 1) for th in range(2)], 0
        )

    def forward(blks):
        sig = jnp.concatenate(blks, 1).astype(BF16)
        spec = dot(a_ref[...], jnp.concatenate([sig, sig], 0))
        re, im = spec[:128], spec[128:]
        t_re, t_im = tr_ref[...], ti_ref[...]
        top, bottom = [], []
        for h in range(2):
            u, w = re[:, h * 256:(h + 1) * 256], im[:, h * 256:(h + 1) * 256]
            top.append(u * t_re - w * t_im)
            bottom.append(u * t_im + w * t_re)
        hi, lo = split(jnp.concatenate(top + bottom, 0))
        full = dot(jnp.concatenate([hi, hi, lo], 1), b_ref[...])
        return full[:256, :256] - full[256:, 256:], full[:256, 256:] + full[256:, :256]

    def inverse(re, im):
        hi, lo = split(jnp.concatenate([re, im], 0))
        full = dot(jnp.concatenate([hi, hi, lo], 1), b_ref[...])
        u = full[:256, :256] + full[256:, 256:]
        w = full[256:, :256] - full[:256, 256:]
        t_re, t_im = tr_ref[...], ti_ref[...]
        top, bottom = [], []
        for h in range(2):
            ur, wi = u[h * 128:(h + 1) * 128], w[h * 128:(h + 1) * 128]
            top.append(ur * t_re + wi * t_im)
            bottom.append(wi * t_re - ur * t_im)
        both = jnp.concatenate([jnp.concatenate(top, 1), jnp.concatenate(bottom, 1)], 0)
        hi, lo = split(both)
        sig = dot(c_ref[...], jnp.concatenate([hi, hi, lo], 0))
        return [sig[:, r * 128:(r + 1) * 128] for r in range(4)]

    loads[0].wait()
    loads[1].wait()
    prod[...] = k_ref[...].astype(F32) * v_ref[...].astype(F32)
    interleave(blocks_of(prod[...]), i4, s0)
    loads[2].wait()
    interleave(blocks_of(taps_ref[...]), i4, s1)
    loads[3].wait()
    loads[4].wait()
    pl.semaphore_wait(bar, NCTX)
    g_send = remote(g_ref, gboth, 9, sibling)
    g_send.start()
    w_send = remote(w_ref.at[:, pl.ds(pl.multiple_of((1 - ch) * 256, 256), 256)], w_oth, 10, sibling)
    w_send.start()
    send_all(s0, r0, 0)
    send_all(s1, r1, 1)

    loads[5].wait()
    g_send.wait_recv()
    mine, other = g_ref[...], gboth[...]
    first = ch == 0
    gfull[:, :256] = jnp.where(first, mine.astype(F32), other.astype(F32)).astype(BF16)
    gfull[:, 256:] = jnp.where(first, other.astype(F32), mine.astype(F32)).astype(BF16)
    dgat[...] = dot(gfull[...], w_ref[...], (((1,), (1,)), ((), ())))
    dmix[...] = dgat[...] * q_ref[...].astype(F32)
    interleave(blocks_of(dmix[...]), i4, s2)
    send_all(s2, r2, 2)

    sk[...] = jnp.broadcast_to(jnp.sum(dmix[...] * prod[...], axis=0, keepdims=True), (8, 256))
    for to in plane_order:
        remote(sk, rsk1.at[plane], 5, at_plane(to)).start()
    for i in range(6, 12):
        loads[i].wait()

    wait_all(s0, r0, 0)
    re, im = forward(separate(r0, i4, 4))
    sig_re[...], sig_im[...] = re, im
    wait_all(s1, r1, 1)
    re, im = forward(separate(r1, i4, 4))
    tap_re[...], tap_im[...] = re, im
    re, im = sig_re[...], sig_im[...]
    conv = inverse(re * tap_re[...] - im * tap_im[...], re * tap_im[...] + im * tap_re[...])
    interleave(conv, i4, s3)
    send_all(s3, r3, 3)

    some(rsk1, 15, 5, at_plane(plane_order[0])).wait_recv()
    rsk1[plane] = sk[...]
    sk2[...] = jnp.sum(rsk1[...], axis=0)
    for to in z_order:
        remote(sk2, rsk2.at[z], 6, at_z(to)).start()

    wait_all(s2, r2, 2)
    re, im = forward(separate(r2, i4, 4))
    lag_p = inverse(re * tap_re[...] + im * tap_im[...], im * tap_re[...] - re * tap_im[...])
    lag_f = inverse(re * sig_re[...] + im * sig_im[...], im * sig_re[...] - re * sig_im[...])
    interleave(lag_p + lag_f, i8, s4)
    send_all(s4, r4, 4)

    wait_all(s3, r3, 3)
    skip = skip_ref[...]
    mixed = tokens_of(separate(r3, i4, 4)) + skip * prod[...]
    gated = (q_ref[...].astype(F32) * mixed).astype(BF16)
    g1[...] = dot(gated, gfull[...], (((0,), (0,)), ((), ()))).astype(BF16)
    for to in plane_order:
        remote(
            g1.at[pl.ds(pl.multiple_of(to * 16, 16), 16)], rg.at[plane], 7, at_plane(to)
        ).start()
    gat_oth[0] = gated
    gat_send = remote(gat_oth.at[0], gat_oth.at[1], 11, sibling)
    gat_send.start()
    gq_ref[...] = (dgat[...] * mixed).astype(BF16)
    w_send.wait_recv()
    w_mine = w_ref[:, pl.ds(pl.multiple_of(ch * 256, 256), 256)]
    part = dot(gated, w_mine)
    gat_send.wait_recv()
    out_ref[...] = (part + dot(gat_oth[1], w_oth[...])).astype(BF16)

    some(rg, 15, 7, at_plane(plane_order[0])).wait_recv()
    rg[plane] = g1[pl.ds(pl.multiple_of(plane * 16, 16), 16), :]
    total = jnp.sum(rg[...].astype(F32), axis=0)
    for i in range(NZ):
        sz[i] = total[i // 4 * 8:i // 4 * 8 + 8, i % 4 * 128:i % 4 * 128 + 128]
    for to in z_order:
        remote(sz.at[to], rz.at[z], 8, at_z(to)).start()
    some(rsk2, 7, 6, at_z(z_order[0])).wait_recv()
    rsk2[z] = sk2[...]
    gs_ref[...] = jnp.sum(rsk2[...], axis=0)[:1] / ROOT
    some(rz, 7, 8, at_z(z_order[0])).wait_recv()
    rz[z] = sz[z]
    az[z] = jnp.sum(rz[...], axis=0) / ROOT
    for to in z_order:
        remote(az.at[z], az.at[z], 12, at_z(to)).start()
    some(az, 7, 12, at_z(z_order[0])).wait_recv()
    rows = [jnp.concatenate([az[4 * i + j] for j in range(4)], 1) for i in range(2)]
    ga[plane] = jnp.concatenate(rows, 0).astype(BF16)
    for to in plane_order:
        remote(ga.at[plane], ga.at[plane], 13, at_plane(to)).start()

    wait_all(s4, r4, 4)
    blks = separate(r4, i8, 8)
    grad_prod = tokens_of(blks[:4]) + skip * dmix[...]
    gk_ref[...] = (grad_prod * v_ref[...].astype(F32)).astype(BF16)
    gv_ref[...] = (grad_prod * k_ref[...].astype(F32)).astype(BF16)
    gf_ref[...] = tokens_of(blks[4:]) / ROOT

    whole(s0, r0, 0).wait_send()
    whole(s1, r1, 1).wait_send()
    whole(s2, r2, 2).wait_send()
    whole(s3, r3, 3).wait_send()
    whole(s4, r4, 4).wait_send()
    some(rsk1, 15, 5, at_plane(plane_order[0])).wait_send()
    some(rsk2, 7, 6, at_z(z_order[0])).wait_send()
    some(rg, 15, 7, at_plane(plane_order[0])).wait_send()
    some(rz, 7, 8, at_z(z_order[0])).wait_send()
    g_send.wait_send()
    w_send.wait_send()
    gat_send.wait_send()
    some(az, 7, 12, at_z(z_order[0])).wait_send()

    last = some(ga, 15, 13, at_plane(plane_order[0]))
    last.wait_recv()
    gw_ref[...] = ga[...].astype(F32).reshape(256, 512)
    last.wait_send()


def finish(*refs):
    count = len(refs) // 2
    for src, dst in zip(refs[:count], refs[count:]):
        dst[...] = src[...]


def shards(query_act, key_act, value_act, filter_taps, skip_gain, out_weight, out_grad):
    a_cat, b_cat, c_cat, t_re, t_im = (jnp.asarray(t) for t in tables())
    vmem = pl.BlockSpec(memory_space=pltpu.VMEM)
    anywhere = pl.BlockSpec(memory_space=pl.ANY)
    sds = jax.ShapeDtypeStruct
    operands = (
        query_act, key_act, value_act, filter_taps, skip_gain[None, :], out_weight, out_grad,
        a_cat, b_cat, c_cat, t_re, t_im,
    )
    results = (
        sds((256, 256), BF16), sds((256, 256), BF16), sds((256, 256), BF16),
        sds((256, 256), BF16), sds((256, 256), F32), sds((1, 256), F32), sds((256, 512), F32),
    )
    msg4, msg8 = pltpu.VMEM((128, 4, 128), BF16), pltpu.VMEM((128, 8, 128), BF16)
    square, half = pltpu.VMEM((256, 256), F32), pltpu.VMEM((256, 256), BF16)
    outs = pl.pallas_call(
        kernel,
        out_shape=results,
        in_specs=[anywhere] * 12,
        out_specs=[vmem] * 7,
        scratch_shapes=[pltpu.VMEM(op.shape, op.dtype) for op in operands] + [
            msg4, msg4, msg4, msg4, msg4, msg4, msg4, msg4, msg8, msg8,
            pltpu.VMEM((1024, 128), F32), pltpu.VMEM((512, 128), F32),
            square, square, square,
            pltpu.VMEM((256, 512), BF16), half, half, pltpu.VMEM((2, 256, 256), BF16),
            square, square, square, square,
            pltpu.VMEM((256, 512), BF16), pltpu.VMEM((16, 16, 512), BF16),
            pltpu.VMEM((8, 8, 128), F32), pltpu.VMEM((8, 8, 128), F32), pltpu.VMEM((8, 8, 128), F32),
            pltpu.VMEM((16, 16, 512), BF16),
            pltpu.VMEM((8, 256), F32), pltpu.VMEM((16, 8, 256), F32),
            pltpu.VMEM((8, 256), F32), pltpu.VMEM((8, 8, 256), F32),
            pltpu.SemaphoreType.DMA((12,)), pltpu.SemaphoreType.DMA((5,)),
            pltpu.SemaphoreType.DMA((14,)), pltpu.SemaphoreType.DMA((14,)),
        ],
        compiler_params=pltpu.CompilerParams(
            collective_id=0, has_side_effects=True, vmem_limit_bytes=56 * 1024 * 1024
        ),
        name="hyena",
    )(*operands)
    outs = pl.pallas_call(
        finish,
        out_shape=results,
        in_specs=[vmem] * 7,
        out_specs=[vmem] * 7,
        name="finish",
    )(*outs)
    out, gq, gk, gv, gf, gs, gw = outs
    return out, gq, gk, gv, gf, gs.reshape(256), gw


def solution(mesh):
    spec = P("ctx", "ch")
    in_specs = (spec, spec, spec, spec, P("ch"), P("ch", None), spec)
    out_specs = (spec, spec, spec, spec, spec, P("ch"), P("ch", None))
    return jax.shard_map(shards, mesh=mesh, in_specs=in_specs, out_specs=out_specs, check_vma=False)
```

time: 72 us -> 59.1 us (0.82)
  local copies, waits for them, and re-layouts: 15.6 us -> 0 us
  Pallas kernels: 54.9 us -> 58.3 us
    unnamed x30 -> x0, local copies, waits for them, and re-layouts: 15.1 us -> none
    pallas_call x1 -> x2, Pallas kernels: 54.9 us -> 58.3 us  [the longest x1 55.9 us: shards(): pl.pallas_call(kernel, out_shape=results, in_specs=[anywhere] * 12, out_s...]
where the time goes in v2:
time: 59.1 us; the launch traced here: 59 us
  Pallas kernels  58.3 us (99%)
  between operations  0.64 us (1%)
    pallas_call x1, Pallas kernels, shards(): pl.pallas_call(kernel, out_shape=results, in_specs=[anywhere] * 12, out_s...  55.9 us
    pallas_call x1, Pallas kernels, shards(): pl.pallas_call(finish, out_shape=results, in_specs=[vmem] * 7, out_specs=...  2.46 us

profile of v2, /device:TPU:2, one launch (start us, length us, event | category | flops | bytes accessed | tf_op | source)
XLA Modules:
  0.0 59.0 jit_solution(11479802203909297416)
XLA Ops:
  0.6 55.9 %hyena.1 = (bf16[256,256]{1,0:T(8,128)(2,1)}, bf16[256,256]{1,0:T(8,128)(2,1)}, bf16[256,256]{1,0:T(8,128)(2,1)}, bf16[256,256]{1,0:T(8,128)(2,1)}, f32[256,256]...) custom-call(bf16[256,256]{1,0:T(8,128)(2,1)} %q_hbm.1, bf16[256,256]{1,0:T(8,128)(2,1)} %k_hbm.1, ...), custom_call_target="tpu_custom_call" | custom-call | tf_op jit(solution)/shard_map/hyena/pallas_call | solution.py:329
  56.5 2.5 %finish.1 = (bf16[256,256]{1,0:T(8,128)(2,1)}, bf16[256,256]{1,0:T(8,128)(2,1)}, bf16[256,256]{1,0:T(8,128)(2,1)}, bf16[256,256]{1,0:T(8,128)(2,1)}, f32[256,256...) custom-call(bf16[256,256]{1,0:T(8,128)(2,1)} %get-tuple-element.21.refs_0_, ...), custom_call_target="tpu_custom_call" | custom-call | tf_op jit(solution)/shard_map/finish/pallas_call | solution.py:353

commit v3 on v2

--- a/solution.py
+++ b/solution.py
@@ -15,6 +15,7 @@
 NY, NZ, NX = 4, 8, 4
 LEN = 32768
 ROOT = math.sqrt(LEN)
+LAG_CUTS = (40, 84)
 
 
 def split_table(table):
@@ -49,10 +50,6 @@
     return hi, (val - hi.astype(F32)).astype(BF16)
 
 
-ORDER4 = (2, 1, 3, 0)
-ORDER8 = (4, 3, 5, 2, 6, 1, 7, 0)
-
-
 def kernel(
     q_hbm, k_hbm, v_hbm, taps_hbm, skip_hbm, w_hbm, g_hbm, a_hbm, b_hbm, c_hbm, tr_hbm, ti_hbm,
     out_ref, gq_ref, gk_ref, gv_ref, gf_ref, gs_ref, gw_ref,
@@ -60,13 +57,41 @@
     s0, r0, s1, r1, s2, r2, s3, r3, s4, r4,
     i8, i4, prod, dmix, dgat, gfull, gboth, w_oth, gat_oth,
     sig_re, sig_im, tap_re, tap_im,
-    g1, rg, sz, rz, az, ga, sk, rsk1, sk2, rsk2,
+    g1, rg, rz, ga, sk, rsk1, sk2, rsk2,
     isem, lsem, ssem, rsem,
 ):
     me = lax.axis_index("ctx")
     ch = lax.axis_index("ch")
     y, z, x = me // 32, lax.rem(me // 4, NZ), lax.rem(me, NX)
     plane = y * NX + x
+
+    def peer(idx):
+        return {"ctx": idx}
+
+    def remote(src, dst, sem, device):
+        return pltpu.make_async_remote_copy(
+            src_ref=src, dst_ref=dst, send_sem=ssem.at[sem], recv_sem=rsem.at[sem],
+            device_id=device, device_id_type=MESH,
+        )
+
+    def at_plane(idx):
+        return peer(idx // NX * 32 + z * NX + lax.rem(idx, NX))
+
+    def at_z(idx):
+        return peer(y * 32 + idx * NX + x)
+
+    plane_order = [lax.rem(plane + step, 16) for step in range(1, 16)]
+    z_order = [lax.rem(z + step, NZ) for step in range(1, NZ)]
+    sibling = {"ch": 1 - ch}
+
+    bar = pltpu.get_barrier_semaphore()
+
+    def greet(step, carry):
+        pl.semaphore_signal(bar, inc=1, device_id=peer(lax.rem(me + 1 + step, NCTX)), device_id_type=MESH)
+        return carry
+
+    lax.fori_loop(0, NCTX - 1, greet, 0)
+    pl.semaphore_signal(bar, inc=1, device_id=sibling, device_id_type=MESH)
 
     loads = {}
     pairs = (
@@ -78,36 +103,6 @@
         loads[i] = pltpu.make_async_copy(src, dst, isem.at[i])
         loads[i].start()
 
-    def peer(idx):
-        return {"ctx": idx}
-
-    def remote(src, dst, sem, device):
-        return pltpu.make_async_remote_copy(
-            src_ref=src, dst_ref=dst, send_sem=ssem.at[sem], recv_sem=rsem.at[sem],
-            device_id=device, device_id_type=MESH,
-        )
-
-    def at_plane(idx):
-        return peer(idx // NX * 32 + z * NX + lax.rem(idx, NX))
-
-    def at_z(idx):
-        return peer(y * 32 + idx * NX + x)
-
-    plane_order = [
-        lax.rem(y + dy, NY) * NX + lax.rem(x + dx, NX) for dy in ORDER4 for dx in ORDER4
-    ][:15]
-    z_order = [lax.rem(z + dz, NZ) for dz in ORDER8][:7]
-    sibling = {"ch": 1 - ch}
-
-    bar = pltpu.get_barrier_semaphore()
-
-    def greet(step, carry):
-        pl.semaphore_signal(bar, inc=1, device_id=peer(lax.rem(me + 1 + step, NCTX)), device_id_type=MESH)
-        return carry
-
-    lax.fori_loop(0, NCTX - 1, greet, 0)
-    pl.semaphore_signal(bar, inc=1, device_id=sibling, device_id_type=MESH)
-
     def interleave(blocks, tmp, dst):
         rows = len(blocks)
         for r, blk in enumerate(blocks):
@@ -118,15 +113,16 @@
         tmp[...] = src[...].astype(F32).reshape(128 * rows, 128)
         return [tmp[pl.ds(r, 128, stride=rows), :] for r in range(rows)]
 
-    def send_all(src, dst, sem):
-        pltpu.make_async_copy(src.at[me], dst.at[me], lsem.at[sem]).start()
+    def send_all(src, dst, sem, low=0, high=NCTX - 1):
+        if low == 0:
+            pltpu.make_async_copy(src.at[me], dst.at[me], lsem.at[sem]).start()
 
         def go(step, carry):
             to = lax.rem(me + 1 + step, NCTX)
             remote(src.at[to], dst.at[me], sem, peer(to)).start()
             return carry
 
-        lax.fori_loop(0, NCTX - 1, go, 0)
+        lax.fori_loop(low, high, go, 0)
 
     def whole(src, dst, sem):
         return remote(
@@ -208,7 +204,7 @@
     interleave(blocks_of(dmix[...]), i4, s2)
     send_all(s2, r2, 2)
 
-    sk[...] = jnp.broadcast_to(jnp.sum(dmix[...] * prod[...], axis=0, keepdims=True), (8, 256))
+    sk[...] = jnp.sum(dmix[...] * prod[...], axis=0, keepdims=True)
     for to in plane_order:
         remote(sk, rsk1.at[plane], 5, at_plane(to)).start()
     for i in range(6, 12):
@@ -236,20 +232,21 @@
     lag_p = inverse(re * tap_re[...] + im * tap_im[...], im * tap_re[...] - re * tap_im[...])
     lag_f = inverse(re * sig_re[...] + im * sig_im[...], im * sig_re[...] - re * sig_im[...])
     interleave(lag_p + lag_f, i8, s4)
-    send_all(s4, r4, 4)
+    if LAG_CUTS[0]:
+        send_all(s4, r4, 4, 0, LAG_CUTS[0])
 
     wait_all(s3, r3, 3)
     skip = skip_ref[...]
     mixed = tokens_of(separate(r3, i4, 4)) + skip * prod[...]
     gated = (q_ref[...].astype(F32) * mixed).astype(BF16)
-    g1[...] = dot(gated, gfull[...], (((0,), (0,)), ((), ()))).astype(BF16)
+    full = dot(gated, gfull[...], (((0,), (0,)), ((), ())))
+    g1[...] = full.reshape(16, 16, 512).astype(BF16)
     for to in plane_order:
-        remote(
-            g1.at[pl.ds(pl.multiple_of(to * 16, 16), 16)], rg.at[plane], 7, at_plane(to)
-        ).start()
+        remote(g1.at[to], rg.at[plane], 7, at_plane(to)).start()
     gat_oth[0] = gated
     gat_send = remote(gat_oth.at[0], gat_oth.at[1], 11, sibling)
     gat_send.start()
+    send_all(s4, r4, 4, LAG_CUTS[0], LAG_CUTS[1])
     gq_ref[...] = (dgat[...] * mixed).astype(BF16)
     w_send.wait_recv()
     w_mine = w_ref[:, pl.ds(pl.multiple_of(ch * 256, 256), 256)]
@@ -258,25 +255,18 @@
     out_ref[...] = (part + dot(gat_oth[1], w_oth[...])).astype(BF16)
 
     some(rg, 15, 7, at_plane(plane_order[0])).wait_recv()
-    rg[plane] = g1[pl.ds(pl.multiple_of(plane * 16, 16), 16), :]
-    total = jnp.sum(rg[...].astype(F32), axis=0)
-    for i in range(NZ):
-        sz[i] = total[i // 4 * 8:i // 4 * 8 + 8, i % 4 * 128:i % 4 * 128 + 128]
+    rg[plane] = g1[plane]
+    rz[z] = jnp.sum(rg[...].astype(F32), axis=0).astype(BF16)
     for to in z_order:
-        remote(sz.at[to], rz.at[z], 8, at_z(to)).start()
+        remote(rz.at[z], rz.at[z], 8, at_z(to)).start()
+    send_all(s4, r4, 4, LAG_CUTS[1], NCTX - 1)
     some(rsk2, 7, 6, at_z(z_order[0])).wait_recv()
     rsk2[z] = sk2[...]
-    gs_ref[...] = jnp.sum(rsk2[...], axis=0)[:1] / ROOT
+    gs_ref[...] = jnp.sum(rsk2[...], axis=0) / ROOT
     some(rz, 7, 8, at_z(z_order[0])).wait_recv()
-    rz[z] = sz[z]
-    az[z] = jnp.sum(rz[...], axis=0) / ROOT
-    for to in z_order:
-        remote(az.at[z], az.at[z], 12, at_z(to)).start()
-    some(az, 7, 12, at_z(z_order[0])).wait_recv()
-    rows = [jnp.concatenate([az[4 * i + j] for j in range(4)], 1) for i in range(2)]
-    ga[plane] = jnp.concatenate(rows, 0).astype(BF16)
+    ga[plane] = (jnp.sum(rz[...].astype(F32), axis=0) / ROOT).astype(BF16)
     for to in plane_order:
-        remote(ga.at[plane], ga.at[plane], 13, at_plane(to)).start()
+        remote(ga.at[plane], ga.at[plane], 12, at_plane(to)).start()
 
     wait_all(s4, r4, 4)
     blks = separate(r4, i8, 8)
@@ -297,18 +287,25 @@
     g_send.wait_send()
     w_send.wait_send()
     gat_send.wait_send()
-    some(az, 7, 12, at_z(z_order[0])).wait_send()
-
-    last = some(ga, 15, 13, at_plane(plane_order[0]))
+
+    last = some(ga, 15, 12, at_plane(plane_order[0]))
     last.wait_recv()
     gw_ref[...] = ga[...].astype(F32).reshape(256, 512)
     last.wait_send()
 
 
 def finish(*refs):
-    count = len(refs) // 2
-    for src, dst in zip(refs[:count], refs[count:]):
-        dst[...] = src[...]
+    count = (len(refs) - 1) // 3
+    src, dst, mid, sem = refs[:count], refs[count:2 * count], refs[2 * count:3 * count], refs[-1]
+    loads = [pltpu.make_async_copy(src[i], mid[i], sem.at[0, i]) for i in range(count)]
+    stores = [pltpu.make_async_copy(mid[i], dst[i], sem.at[1, i]) for i in range(count)]
+    for one in loads:
+        one.start()
+    for load, store in zip(loads, stores):
+        load.wait()
+        store.start()
+    for one in stores:
+        one.wait()
 
 
 def shards(query_act, key_act, value_act, filter_taps, skip_gain, out_weight, out_grad):
@@ -337,13 +334,12 @@
             square, square, square,
             pltpu.VMEM((256, 512), BF16), half, half, pltpu.VMEM((2, 256, 256), BF16),
             square, square, square, square,
-            pltpu.VMEM((256, 512), BF16), pltpu.VMEM((16, 16, 512), BF16),
-            pltpu.VMEM((8, 8, 128), F32), pltpu.VMEM((8, 8, 128), F32), pltpu.VMEM((8, 8, 128), F32),
-            pltpu.VMEM((16, 16, 512), BF16),
-            pltpu.VMEM((8, 256), F32), pltpu.VMEM((16, 8, 256), F32),
-            pltpu.VMEM((8, 256), F32), pltpu.VMEM((8, 8, 256), F32),
+            pltpu.VMEM((16, 16, 512), BF16), pltpu.VMEM((16, 16, 512), BF16),
+            pltpu.VMEM((8, 16, 512), BF16), pltpu.VMEM((16, 16, 512), BF16),
+            pltpu.VMEM((1, 256), F32), pltpu.VMEM((16, 1, 256), F32),
+            pltpu.VMEM((1, 256), F32), pltpu.VMEM((8, 1, 256), F32),
             pltpu.SemaphoreType.DMA((12,)), pltpu.SemaphoreType.DMA((5,)),
-            pltpu.SemaphoreType.DMA((14,)), pltpu.SemaphoreType.DMA((14,)),
+            pltpu.SemaphoreType.DMA((13,)), pltpu.SemaphoreType.DMA((13,)),
         ],
         compiler_params=pltpu.CompilerParams(
             collective_id=0, has_side_effects=True, vmem_limit_bytes=56 * 1024 * 1024
@@ -353,8 +349,10 @@
     outs = pl.pallas_call(
         finish,
         out_shape=results,
-        in_specs=[vmem] * 7,
-        out_specs=[vmem] * 7,
+        in_specs=[anywhere] * 7,
+        out_specs=[anywhere] * 7,
+        scratch_shapes=[pltpu.VMEM(res.shape, res.dtype) for res in results]
+        + [pltpu.SemaphoreType.DMA((2, 7))],
         name="finish",
     )(*outs)
     out, gq, gk, gv, gf, gs, gw = outs

time: 59.1 us -> 55.7 us (0.942)
  Pallas kernels: 58.3 us -> 54.4 us
    pallas_call x1, Pallas kernels: 55.9 us -> 52.1 us  [shards(): pl.pallas_call(kernel, out_shape=results, in_specs=[anywhere] * 12, out_s...]
where the time goes in v3:
time: 55.7 us; the launch traced here: 55 us
  Pallas kernels  54.4 us (98%)
  between operations  0.64 us (1%)
    pallas_call x1, Pallas kernels, shards(): pl.pallas_call(kernel, out_shape=results, in_specs=[anywhere] * 12, out_s...  52.1 us
    pallas_call x1, Pallas kernels, shards(): pl.pallas_call(finish, out_shape=results, in_specs=[anywhere] * 7, out_sp...  2.31 us

profile of v3, /device:TPU:2, one launch (start us, length us, event | category | flops | bytes accessed | tf_op | source)
XLA Modules:
  0.0 55.0 jit_solution(2485912597093537131)
XLA Ops:
  0.6 52.1 %hyena.1 = (bf16[256,256]{1,0:T(8,128)(2,1)}, bf16[256,256]{1,0:T(8,128)(2,1)}, bf16[256,256]{1,0:T(8,128)(2,1)}, bf16[256,256]{1,0:T(8,128)(2,1)}, f32[256,256]...) custom-call(bf16[256,256]{1,0:T(8,128)(2,1)} %q_hbm.1, bf16[256,256]{1,0:T(8,128)(2,1)} %k_hbm.1, ...), custom_call_target="tpu_custom_call" | custom-call | tf_op jit(solution)/shard_map/hyena/pallas_call | solution.py:326
  52.7 2.3 %finish.1 = (bf16[256,256]{1,0:T(8,128)(2,1)}, bf16[256,256]{1,0:T(8,128)(2,1)}, bf16[256,256]{1,0:T(8,128)(2,1)}, bf16[256,256]{1,0:T(8,128)(2,1)}, f32[256,256...) custom-call(bf16[256,256]{1,0:T(8,128)(2,1)} %get-tuple-element.21.refs_0_, ...), custom_call_target="tpu_custom_call" | custom-call | tf_op jit(solution)/shard_map/finish/pallas_call | solution.py:349

commit v4 on v3

--- a/solution.py
+++ b/solution.py
@@ -15,7 +15,10 @@
 NY, NZ, NX = 4, 8, 4
 LEN = 32768
 ROOT = math.sqrt(LEN)
-LAG_CUTS = (40, 84)
+LAG_CUTS = (64, 127)
+PARTS = 4
+WIDTH = 512 // PARTS
+SCATTER, ACROSS, GATHER = (7, 13, 16, 17), (8, 14, 18, 19), (12, 15, 20, 21)
 
 
 def split_table(table):
@@ -52,13 +55,14 @@
 
 def kernel(
     q_hbm, k_hbm, v_hbm, taps_hbm, skip_hbm, w_hbm, g_hbm, a_hbm, b_hbm, c_hbm, tr_hbm, ti_hbm,
-    out_ref, gq_ref, gk_ref, gv_ref, gf_ref, gs_ref, gw_ref,
+    out_hbm, gq_hbm, gk_hbm, gv_hbm, gf_hbm, gs_hbm, gw_hbm,
     q_ref, k_ref, v_ref, taps_ref, skip_ref, w_ref, g_ref, a_ref, b_ref, c_ref, tr_ref, ti_ref,
     s0, r0, s1, r1, s2, r2, s3, r3, s4, r4,
     i8, i4, prod, dmix, dgat, gfull, gboth, w_oth, gat_oth,
     sig_re, sig_im, tap_re, tap_im,
     g1, rg, rz, ga, sk, rsk1, sk2, rsk2,
-    isem, lsem, ssem, rsem,
+    out_ref, gq_ref, gk_ref, gv_ref, gf_ref, gs_ref,
+    isem, osem, lsem, ssem, rsem,
 ):
     me = lax.axis_index("ctx")
     ch = lax.axis_index("ch")
@@ -86,11 +90,12 @@
 
     bar = pltpu.get_barrier_semaphore()
 
-    def greet(step, carry):
-        pl.semaphore_signal(bar, inc=1, device_id=peer(lax.rem(me + 1 + step, NCTX)), device_id_type=MESH)
+    def greet(to, carry):
+        pl.semaphore_signal(bar, inc=1, device_id=peer(to), device_id_type=MESH)
         return carry
 
-    lax.fori_loop(0, NCTX - 1, greet, 0)
+    lax.fori_loop(me + 1, NCTX, greet, 0)
+    lax.fori_loop(0, me, greet, 0)
     pl.semaphore_signal(bar, inc=1, device_id=sibling, device_id_type=MESH)
 
     loads = {}
@@ -117,12 +122,15 @@
         if low == 0:
             pltpu.make_async_copy(src.at[me], dst.at[me], lsem.at[sem]).start()
 
-        def go(step, carry):
-            to = lax.rem(me + 1 + step, NCTX)
+        def go(to, carry):
             remote(src.at[to], dst.at[me], sem, peer(to)).start()
             return carry
 
-        lax.fori_loop(low, high, go, 0)
+        if (low, high) == (0, NCTX - 1):
+            lax.fori_loop(me + 1, NCTX, go, 0)
+            lax.fori_loop(0, me, go, 0)
+        else:
+            lax.fori_loop(low, high, lambda step, carry: go(lax.rem(me + 1 + step, NCTX), carry), 0)
 
     def whole(src, dst, sem):
         return remote(
@@ -136,6 +144,17 @@
     def some(buf, count, sem, device):
         part = buf.at[pl.ds(0, count)]
         return remote(part, part, sem, device)
+
+    def some_half(buf, h, count, sem, device):
+        part = buf.at[h, pl.ds(0, count)]
+        return remote(part, part, sem, device)
+
+    stores = []
+
+    def store(src, dst):
+        one = pltpu.make_async_copy(src, dst, osem.at[len(stores)])
+        one.start()
+        stores.append(one)
 
     def blocks_of(val):
         return [
@@ -239,41 +258,50 @@
     skip = skip_ref[...]
     mixed = tokens_of(separate(r3, i4, 4)) + skip * prod[...]
     gated = (q_ref[...].astype(F32) * mixed).astype(BF16)
-    full = dot(gated, gfull[...], (((0,), (0,)), ((), ())))
-    g1[...] = full.reshape(16, 16, 512).astype(BF16)
-    for to in plane_order:
-        remote(g1.at[to], rg.at[plane], 7, at_plane(to)).start()
+    for h in range(PARTS):
+        full = dot(gated, gfull[:, h * WIDTH:(h + 1) * WIDTH], (((0,), (0,)), ((), ())))
+        g1[h] = full.reshape(16, 16, WIDTH).astype(BF16)
+        for to in plane_order:
+            remote(g1.at[h, to], rg.at[h, plane], SCATTER[h], at_plane(to)).start()
     gat_oth[0] = gated
     gat_send = remote(gat_oth.at[0], gat_oth.at[1], 11, sibling)
     gat_send.start()
     send_all(s4, r4, 4, LAG_CUTS[0], LAG_CUTS[1])
     gq_ref[...] = (dgat[...] * mixed).astype(BF16)
+    store(gq_ref, gq_hbm)
     w_send.wait_recv()
     w_mine = w_ref[:, pl.ds(pl.multiple_of(ch * 256, 256), 256)]
     part = dot(gated, w_mine)
     gat_send.wait_recv()
     out_ref[...] = (part + dot(gat_oth[1], w_oth[...])).astype(BF16)
-
-    some(rg, 15, 7, at_plane(plane_order[0])).wait_recv()
-    rg[plane] = g1[plane]
-    rz[z] = jnp.sum(rg[...].astype(F32), axis=0).astype(BF16)
-    for to in z_order:
-        remote(rz.at[z], rz.at[z], 8, at_z(to)).start()
+    store(out_ref, out_hbm)
+
+    for h in range(PARTS):
+        some_half(rg, h, 15, SCATTER[h], at_plane(plane_order[0])).wait_recv()
+        rg[h, plane] = g1[h, plane]
+        rz[h, z] = jnp.sum(rg[h].astype(F32), axis=0).astype(BF16)
+        for to in z_order:
+            remote(rz.at[h, z], rz.at[h, z], ACROSS[h], at_z(to)).start()
     send_all(s4, r4, 4, LAG_CUTS[1], NCTX - 1)
     some(rsk2, 7, 6, at_z(z_order[0])).wait_recv()
     rsk2[z] = sk2[...]
     gs_ref[...] = jnp.sum(rsk2[...], axis=0) / ROOT
-    some(rz, 7, 8, at_z(z_order[0])).wait_recv()
-    ga[plane] = (jnp.sum(rz[...].astype(F32), axis=0) / ROOT).astype(BF16)
-    for to in plane_order:
-        remote(ga.at[plane], ga.at[plane], 12, at_plane(to)).start()
+    store(gs_ref, gs_hbm)
+    for h in range(PARTS):
+        some_half(rz, h, 7, ACROSS[h], at_z(z_order[0])).wait_recv()
+        ga[h, plane] = (jnp.sum(rz[h].astype(F32), axis=0) / ROOT).astype(BF16)
+        for to in plane_order:
+            remote(ga.at[h, plane], ga.at[h, plane], GATHER[h], at_plane(to)).start()
 
     wait_all(s4, r4, 4)
     blks = separate(r4, i8, 8)
     grad_prod = tokens_of(blks[:4]) + skip * dmix[...]
     gk_ref[...] = (grad_prod * v_ref[...].astype(F32)).astype(BF16)
     gv_ref[...] = (grad_prod * k_ref[...].astype(F32)).astype(BF16)
-    gf_ref[...] = tokens_of(blks[4:]) / ROOT
+    gf_ref[...] = tokens_of(blks[4:]).astype(BF16)
+    store(gk_ref, gk_hbm)
+    store(gv_ref, gv_hbm)
+    store(gf_ref, gf_hbm)
 
     whole(s0, r0, 0).wait_send()
     whole(s1, r1, 1).wait_send()
@@ -282,35 +310,44 @@
     whole(s4, r4, 4).wait_send()
     some(rsk1, 15, 5, at_plane(plane_order[0])).wait_send()
     some(rsk2, 7, 6, at_z(z_order[0])).wait_send()
-    some(rg, 15, 7, at_plane(plane_order[0])).wait_send()
-    some(rz, 7, 8, at_z(z_order[0])).wait_send()
+    for h in range(PARTS):
+        some_half(rg, h, 15, SCATTER[h], at_plane(plane_order[0])).wait_send()
+        some_half(rz, h, 7, ACROSS[h], at_z(z_order[0])).wait_send()
     g_send.wait_send()
     w_send.wait_send()
     gat_send.wait_send()
 
-    last = some(ga, 15, 12, at_plane(plane_order[0]))
-    last.wait_recv()
-    gw_ref[...] = ga[...].astype(F32).reshape(256, 512)
-    last.wait_send()
-
-
-def finish(*refs):
-    count = (len(refs) - 1) // 3
-    src, dst, mid, sem = refs[:count], refs[count:2 * count], refs[2 * count:3 * count], refs[-1]
-    loads = [pltpu.make_async_copy(src[i], mid[i], sem.at[0, i]) for i in range(count)]
-    stores = [pltpu.make_async_copy(mid[i], dst[i], sem.at[1, i]) for i in range(count)]
-    for one in loads:
-        one.start()
-    for load, store in zip(loads, stores):
-        load.wait()
-        store.start()
+    for h in range(PARTS):
+        last = some_half(ga, h, 15, GATHER[h], at_plane(plane_order[0]))
+        last.wait_recv()
+        store(ga.at[h], gw_hbm.at[h])
+        last.wait_send()
     for one in stores:
         one.wait()
 
 
+def finish(*refs):
+    src, dst, mid, taps, wide, sem = refs[:7], refs[7:14], refs[14:21], refs[21], refs[22], refs[23]
+    last = list(mid[:4]) + [taps, mid[5], wide]
+    loads = [pltpu.make_async_copy(src[i], mid[i], sem.at[0, i]) for i in range(7)]
+    stores = [pltpu.make_async_copy(last[i], dst[i], sem.at[1, i]) for i in range(7)]
+    order = (0, 6, 4, 1, 2, 3, 5)
+    for i in order:
+        loads[i].start()
+    for i in order:
+        loads[i].wait()
+        if i == 6:
+            for h in range(PARTS):
+                wide[:, h * WIDTH:(h + 1) * WIDTH] = mid[6][h].astype(F32).reshape(256, WIDTH)
+        if i == 4:
+            taps[...] = mid[4][...].astype(F32) / ROOT
+        stores[i].start()
+    for one in stores:
+        one.wait()
+
+
 def shards(query_act, key_act, value_act, filter_taps, skip_gain, out_weight, out_grad):
     a_cat, b_cat, c_cat, t_re, t_im = (jnp.asarray(t) for t in tables())
-    vmem = pl.BlockSpec(memory_space=pltpu.VMEM)
     anywhere = pl.BlockSpec(memory_space=pl.ANY)
     sds = jax.ShapeDtypeStruct
     operands = (
@@ -323,23 +360,26 @@
     )
     msg4, msg8 = pltpu.VMEM((128, 4, 128), BF16), pltpu.VMEM((128, 8, 128), BF16)
     square, half = pltpu.VMEM((256, 256), F32), pltpu.VMEM((256, 256), BF16)
+    halves = sds((PARTS, 16, 16, WIDTH), BF16)
+    middle = results[:4] + (sds((256, 256), BF16), results[5], halves)
     outs = pl.pallas_call(
         kernel,
-        out_shape=results,
+        out_shape=middle,
         in_specs=[anywhere] * 12,
-        out_specs=[vmem] * 7,
+        out_specs=[anywhere] * 7,
         scratch_shapes=[pltpu.VMEM(op.shape, op.dtype) for op in operands] + [
             msg4, msg4, msg4, msg4, msg4, msg4, msg4, msg4, msg8, msg8,
             pltpu.VMEM((1024, 128), F32), pltpu.VMEM((512, 128), F32),
             square, square, square,
             pltpu.VMEM((256, 512), BF16), half, half, pltpu.VMEM((2, 256, 256), BF16),
             square, square, square, square,
-            pltpu.VMEM((16, 16, 512), BF16), pltpu.VMEM((16, 16, 512), BF16),
-            pltpu.VMEM((8, 16, 512), BF16), pltpu.VMEM((16, 16, 512), BF16),
+            pltpu.VMEM((PARTS, 16, 16, WIDTH), BF16), pltpu.VMEM((PARTS, 16, 16, WIDTH), BF16),
+            pltpu.VMEM((PARTS, 8, 16, WIDTH), BF16), pltpu.VMEM((PARTS, 16, 16, WIDTH), BF16),
             pltpu.VMEM((1, 256), F32), pltpu.VMEM((16, 1, 256), F32),
             pltpu.VMEM((1, 256), F32), pltpu.VMEM((8, 1, 256), F32),
-            pltpu.SemaphoreType.DMA((12,)), pltpu.SemaphoreType.DMA((5,)),
-            pltpu.SemaphoreType.DMA((13,)), pltpu.SemaphoreType.DMA((13,)),
+            half, half, half, half, half, pltpu.VMEM((1, 256), F32),
+            pltpu.SemaphoreType.DMA((12,)), pltpu.SemaphoreType.DMA((12,)), pltpu.SemaphoreType.DMA((5,)),
+            pltpu.SemaphoreType.DMA((22,)), pltpu.SemaphoreType.DMA((22,)),
         ],
         compiler_params=pltpu.CompilerParams(
             collective_id=0, has_side_effects=True, vmem_limit_bytes=56 * 1024 * 1024
@@ -351,8 +391,8 @@
         out_shape=results,
         in_specs=[anywhere] * 7,
         out_specs=[anywhere] * 7,
-        scratch_shapes=[pltpu.VMEM(res.shape, res.dtype) for res in results]
-        + [pltpu.SemaphoreType.DMA((2, 7))],
+        scratch_shapes=[pltpu.VMEM(res.shape, res.dtype) for res in middle]
+        + [pltpu.VMEM((256, 256), F32), pltpu.VMEM((256, 512), F32), pltpu.SemaphoreType.DMA((2, 7))],
         name="finish",
     )(*outs)
     out, gq, gk, gv, gf, gs, gw = outs

time: 55.7 us -> 53.3 us (0.957)
  Pallas kernels: 54.4 us -> 52.4 us
    pallas_call x1, Pallas kernels: 52.1 us -> 50.2 us  [shards(): pl.pallas_call(kernel, out_shape=middle, in_specs=[anywhere] * 12, out_sp...]
where the time goes in v4:
time: 53.3 us; the launch traced here: 53.1 us
  Pallas kernels  52.4 us (98%)
  between operations  0.64 us (1%)
    pallas_call x1, Pallas kernels, shards(): pl.pallas_call(kernel, out_shape=middle, in_specs=[anywhere] * 12, out_sp...  50.2 us
    pallas_call x1, Pallas kernels, shards(): pl.pallas_call(finish, out_shape=results, in_specs=[anywhere] * 7, out_sp...  2.21 us

profile of v4, /device:TPU:2, one launch (start us, length us, event | category | flops | bytes accessed | tf_op | source)
XLA Modules:
  0.0 53.1 jit_solution(12624555880784370020)
XLA Ops:
  0.6 50.2 %hyena.1 = (bf16[256,256]{1,0:T(8,128)(2,1)}, bf16[256,256]{1,0:T(8,128)(2,1)}, bf16[256,256]{1,0:T(8,128)(2,1)}, bf16[256,256]{1,0:T(8,128)(2,1)}, bf16[256,256...) custom-call(bf16[256,256]{1,0:T(8,128)(2,1)} %q_hbm.1, bf16[256,256]{1,0:T(8,128)(2,1)} %k_hbm.1, ...), custom_call_target="tpu_custom_call" | custom-call | tf_op jit(solution)/shard_map/hyena/pallas_call | solution.py:365
  50.9 2.2 %finish.1 = (bf16[256,256]{1,0:T(8,128)(2,1)}, bf16[256,256]{1,0:T(8,128)(2,1)}, bf16[256,256]{1,0:T(8,128)(2,1)}, bf16[256,256]{1,0:T(8,128)(2,1)}, f32[256,256...) custom-call(bf16[256,256]{1,0:T(8,128)(2,1)} %get-tuple-element.21.refs_0_, ...), custom_call_target="tpu_custom_call" | custom-call | tf_op jit(solution)/shard_map/finish/pallas_call | solution.py:389

commit v5 on v4

--- a/solution.py
+++ b/solution.py
@@ -39,7 +39,8 @@
     tw = -2 * np.pi * ((n2[None, :] * (4 * n1[:, None] + 1)) % (4 * LEN)) / (4 * LEN)
     t_re, t_im = np.cos(tw).astype(np.float32), np.sin(tw).astype(np.float32)
     bang = -2 * np.pi * ((n2[:, None] * n2[None, :]) % 256) / 256
-    b_hi, b_lo = split_table(np.concatenate([np.cos(bang), np.sin(bang)], 1))
+    b_re, b_im = np.cos(bang), np.sin(bang)
+    b_hi, b_lo = split_table(np.block([[b_re, b_im], [-b_im, b_re]]))
     b_cat = np.concatenate([b_hi, b_lo, b_hi], 0)
     return a_cat, b_cat, c_cat, t_re, t_im
 
@@ -58,7 +59,7 @@
     out_hbm, gq_hbm, gk_hbm, gv_hbm, gf_hbm, gs_hbm, gw_hbm,
     q_ref, k_ref, v_ref, taps_ref, skip_ref, w_ref, g_ref, a_ref, b_ref, c_ref, tr_ref, ti_ref,
     s0, r0, s1, r1, s2, r2, s3, r3, s4, r4,
-    i8, i4, prod, dmix, dgat, gfull, gboth, w_oth, gat_oth,
+    i8, i4, prod, dmix, dgat, base_t, q_t, gfull, gboth, w_oth, gat_oth,
     sig_re, sig_im, tap_re, tap_im,
     g1, rg, rz, ga, sk, rsk1, sk2, rsk2,
     out_ref, gq_ref, gk_ref, gv_ref, gf_ref, gs_ref,
@@ -161,10 +162,19 @@
             val[th * 128:(th + 1) * 128, h * 128:(h + 1) * 128].T for h in range(2) for th in range(2)
         ]
 
+    def channels_of(blks):
+        return jnp.concatenate(
+            [jnp.concatenate([blks[2 * h], blks[2 * h + 1]], 1) for h in range(2)], 0
+        )
+
     def tokens_of(blks):
         return jnp.concatenate(
             [jnp.concatenate([blks[th].T, blks[2 + th].T], 1) for th in range(2)], 0
         )
+
+    def rotate(left, right):
+        (lh, ll), (rh, rl) = split(left), split(right)
+        return dot(jnp.concatenate([lh, rh, lh, rh, ll, rl], 1), b_ref[...])
 
     def forward(blks):
         sig = jnp.concatenate(blks, 1).astype(BF16)
@@ -176,15 +186,12 @@
             u, w = re[:, h * 256:(h + 1) * 256], im[:, h * 256:(h + 1) * 256]
             top.append(u * t_re - w * t_im)
             bottom.append(u * t_im + w * t_re)
-        hi, lo = split(jnp.concatenate(top + bottom, 0))
-        full = dot(jnp.concatenate([hi, hi, lo], 1), b_ref[...])
-        return full[:256, :256] - full[256:, 256:], full[:256, 256:] + full[256:, :256]
+        full = rotate(jnp.concatenate(top, 0), jnp.concatenate(bottom, 0))
+        return full[:, :256], full[:, 256:]
 
     def inverse(re, im):
-        hi, lo = split(jnp.concatenate([re, im], 0))
-        full = dot(jnp.concatenate([hi, hi, lo], 1), b_ref[...])
-        u = full[:256, :256] + full[256:, 256:]
-        w = full[256:, :256] - full[:256, 256:]
+        full = rotate(im, re)
+        u, w = full[:, 256:], full[:, :256]
         t_re, t_im = tr_ref[...], ti_ref[...]
         top, bottom = [], []
         for h in range(2):
@@ -221,12 +228,15 @@
     dgat[...] = dot(gfull[...], w_ref[...], (((1,), (1,)), ((), ())))
     dmix[...] = dgat[...] * q_ref[...].astype(F32)
     interleave(blocks_of(dmix[...]), i4, s2)
+    loads[11].wait()
+    base_t[...] = channels_of(blocks_of(skip_ref[...] * prod[...]))
+    q_t[...] = channels_of(blocks_of(q_ref[...].astype(F32)))
     send_all(s2, r2, 2)
 
     sk[...] = jnp.sum(dmix[...] * prod[...], axis=0, keepdims=True)
     for to in plane_order:
         remote(sk, rsk1.at[plane], 5, at_plane(to)).start()
-    for i in range(6, 12):
+    for i in range(6, 11):
         loads[i].wait()
 
     wait_all(s0, r0, 0)
@@ -255,25 +265,28 @@
         send_all(s4, r4, 4, 0, LAG_CUTS[0])
 
     wait_all(s3, r3, 3)
-    skip = skip_ref[...]
-    mixed = tokens_of(separate(r3, i4, 4)) + skip * prod[...]
-    gated = (q_ref[...].astype(F32) * mixed).astype(BF16)
-    for h in range(PARTS):
-        full = dot(gated, gfull[:, h * WIDTH:(h + 1) * WIDTH], (((0,), (0,)), ((), ())))
+    mixed_t = channels_of(separate(r3, i4, 4)) + base_t[...]
+    gated_t = (q_t[...] * mixed_t).astype(BF16)
+    for h in range(PARTS):
+        full = dot(gated_t, gfull[:, h * WIDTH:(h + 1) * WIDTH])
         g1[h] = full.reshape(16, 16, WIDTH).astype(BF16)
         for to in plane_order:
             remote(g1.at[h, to], rg.at[h, plane], SCATTER[h], at_plane(to)).start()
-    gat_oth[0] = gated
+    gat_oth[0] = gated_t
     gat_send = remote(gat_oth.at[0], gat_oth.at[1], 11, sibling)
     gat_send.start()
     send_all(s4, r4, 4, LAG_CUTS[0], LAG_CUTS[1])
+    mixed = tokens_of(
+        [mixed_t[h * 128:(h + 1) * 128, th * 128:(th + 1) * 128] for h in range(2) for th in range(2)]
+    )
     gq_ref[...] = (dgat[...] * mixed).astype(BF16)
     store(gq_ref, gq_hbm)
     w_send.wait_recv()
     w_mine = w_ref[:, pl.ds(pl.multiple_of(ch * 256, 256), 256)]
-    part = dot(gated, w_mine)
+    turned = (((0,), (0,)), ((), ()))
+    part = dot(gated_t, w_mine, turned)
     gat_send.wait_recv()
-    out_ref[...] = (part + dot(gat_oth[1], w_oth[...])).astype(BF16)
+    out_ref[...] = (part + dot(gat_oth[1], w_oth[...], turned)).astype(BF16)
     store(out_ref, out_hbm)
 
     for h in range(PARTS):
@@ -295,7 +308,7 @@
 
     wait_all(s4, r4, 4)
     blks = separate(r4, i8, 8)
-    grad_prod = tokens_of(blks[:4]) + skip * dmix[...]
+    grad_prod = tokens_of(blks[:4]) + skip_ref[...] * dmix[...]
     gk_ref[...] = (grad_prod * v_ref[...].astype(F32)).astype(BF16)
     gv_ref[...] = (grad_prod * k_ref[...].astype(F32)).astype(BF16)
     gf_ref[...] = tokens_of(blks[4:]).astype(BF16)
@@ -328,21 +341,31 @@
 
 def finish(*refs):
     src, dst, mid, taps, wide, sem = refs[:7], refs[7:14], refs[14:21], refs[21], refs[22], refs[23]
-    last = list(mid[:4]) + [taps, mid[5], wide]
-    loads = [pltpu.make_async_copy(src[i], mid[i], sem.at[0, i]) for i in range(7)]
-    stores = [pltpu.make_async_copy(last[i], dst[i], sem.at[1, i]) for i in range(7)]
-    order = (0, 6, 4, 1, 2, 3, 5)
-    for i in order:
-        loads[i].start()
-    for i in order:
+    last = list(mid[:4]) + [taps, mid[5]]
+    columns = [slice(h * WIDTH, (h + 1) * WIDTH) for h in range(PARTS)]
+    loads = [pltpu.make_async_copy(src[i], mid[i], sem.at[0, i]) for i in range(6)]
+    parts = [
+        pltpu.make_async_copy(src[6].at[h], mid[6].at[h], sem.at[0, 6 + h]) for h in range(PARTS)
+    ]
+    stores = [pltpu.make_async_copy(last[i], dst[i], sem.at[1, i]) for i in range(6)]
+    outs = [
+        pltpu.make_async_copy(wide.at[:, columns[h]], dst[6].at[:, columns[h]], sem.at[1, 6 + h])
+        for h in range(PARTS)
+    ]
+    for one in parts[:2] + [loads[4]] + parts[2:] + loads[:4] + [loads[5]]:
+        one.start()
+    for h in range(PARTS):
+        parts[h].wait()
+        wide[:, columns[h]] = mid[6][h].astype(F32).reshape(256, WIDTH)
+        outs[h].start()
+        if h == 1:
+            loads[4].wait()
+            taps[...] = mid[4][...].astype(F32) / ROOT
+            stores[4].start()
+    for i in (0, 1, 2, 3, 5):
         loads[i].wait()
-        if i == 6:
-            for h in range(PARTS):
-                wide[:, h * WIDTH:(h + 1) * WIDTH] = mid[6][h].astype(F32).reshape(256, WIDTH)
-        if i == 4:
-            taps[...] = mid[4][...].astype(F32) / ROOT
         stores[i].start()
-    for one in stores:
+    for one in stores + outs:
         one.wait()
 
 
@@ -370,7 +393,7 @@
         scratch_shapes=[pltpu.VMEM(op.shape, op.dtype) for op in operands] + [
             msg4, msg4, msg4, msg4, msg4, msg4, msg4, msg4, msg8, msg8,
             pltpu.VMEM((1024, 128), F32), pltpu.VMEM((512, 128), F32),
-            square, square, square,
+            square, square, square, square, square,
             pltpu.VMEM((256, 512), BF16), half, half, pltpu.VMEM((2, 256, 256), BF16),
             square, square, square, square,
             pltpu.VMEM((PARTS, 16, 16, WIDTH), BF16), pltpu.VMEM((PARTS, 16, 16, WIDTH), BF16),
@@ -392,7 +415,7 @@
         in_specs=[anywhere] * 7,
         out_specs=[anywhere] * 7,
         scratch_shapes=[pltpu.VMEM(res.shape, res.dtype) for res in middle]
-        + [pltpu.VMEM((256, 256), F32), pltpu.VMEM((256, 512), F32), pltpu.SemaphoreType.DMA((2, 7))],
+        + [pltpu.VMEM((256, 256), F32), pltpu.VMEM((256, 512), F32), pltpu.SemaphoreType.DMA((2, 6 + PARTS))],
         name="finish",
     )(*outs)
     out, gq, gk, gv, gf, gs, gw = outs

time: 53.3 us -> 52.7 us (0.989)
  Pallas kernels: 52.4 us -> 51.5 us
    pallas_call x1, Pallas kernels: 50.2 us -> 49.4 us  [shards(): pl.pallas_call(kernel, out_shape=middle, in_specs=[anywhere] * 12, out_sp...]
where the time goes in v5:
time: 52.7 us; the launch traced here: 52.1 us
  Pallas kernels  51.5 us (98%)
  between operations  0.64 us (1%)
    pallas_call x1, Pallas kernels, shards(): pl.pallas_call(kernel, out_shape=middle, in_specs=[anywhere] * 12, out_sp...  49.4 us
    pallas_call x1, Pallas kernels, shards(): pl.pallas_call(finish, out_shape=results, in_specs=[anywhere] * 7, out_sp...  2.14 us

profile of v5, /device:TPU:2, one launch (start us, length us, event | category | flops | bytes accessed | tf_op | source)
XLA Modules:
  0.0 52.1 jit_solution(15608615269881607866)
XLA Ops:
  0.6 49.4 %hyena.1 = (bf16[256,256]{1,0:T(8,128)(2,1)}, bf16[256,256]{1,0:T(8,128)(2,1)}, bf16[256,256]{1,0:T(8,128)(2,1)}, bf16[256,256]{1,0:T(8,128)(2,1)}, bf16[256,256...) custom-call(bf16[256,256]{1,0:T(8,128)(2,1)} %q_hbm.1, bf16[256,256]{1,0:T(8,128)(2,1)} %k_hbm.1, ...), custom_call_target="tpu_custom_call" | custom-call | tf_op jit(solution)/shard_map/hyena/pallas_call | solution.py:388
  50.0 2.1 %finish.1 = (bf16[256,256]{1,0:T(8,128)(2,1)}, bf16[256,256]{1,0:T(8,128)(2,1)}, bf16[256,256]{1,0:T(8,128)(2,1)}, bf16[256,256]{1,0:T(8,128)(2,1)}, f32[256,256...) custom-call(bf16[256,256]{1,0:T(8,128)(2,1)} %get-tuple-element.21.refs_0_, ...), custom_call_target="tpu_custom_call" | custom-call | tf_op jit(solution)/shard_map/finish/pallas_call | solution.py:412

commit v6 on v5

--- a/solution.py
+++ b/solution.py
@@ -268,8 +268,10 @@
     mixed_t = channels_of(separate(r3, i4, 4)) + base_t[...]
     gated_t = (q_t[...] * mixed_t).astype(BF16)
     for h in range(PARTS):
-        full = dot(gated_t, gfull[:, h * WIDTH:(h + 1) * WIDTH])
-        g1[h] = full.reshape(16, 16, WIDTH).astype(BF16)
+        if h % 2 == 0:
+            full = dot(gated_t, gfull[:, h * WIDTH:(h + 2) * WIDTH])
+        part = full[:, h % 2 * WIDTH:(h % 2 + 1) * WIDTH]
+        g1[h] = part.reshape(16, 16, WIDTH).astype(BF16)
         for to in plane_order:
             remote(g1.at[h, to], rg.at[h, plane], SCATTER[h], at_plane(to)).start()
     gat_oth[0] = gated_t

time: 52.7 us -> 52.8 us (level)
  no operation moved by 1% of the time
where the time goes in v6:
time: 52.8 us; the launch traced here: 52.1 us
  Pallas kernels  51.5 us (98%)
  between operations  0.64 us (1%)
    pallas_call x1, Pallas kernels, shards(): pl.pallas_call(kernel, out_shape=middle, in_specs=[anywhere] * 12, out_sp...  49.3 us
    pallas_call x1, Pallas kernels, shards(): pl.pallas_call(finish, out_shape=results, in_specs=[anywhere] * 7, out_sp...  2.14 us

profile of v6, /device:TPU:2, one launch (start us, length us, event | category | flops | bytes accessed | tf_op | source)
XLA Modules:
  0.0 52.1 jit_solution(9616781619029777608)
XLA Ops:
  0.6 49.3 %hyena.1 = (bf16[256,256]{1,0:T(8,128)(2,1)}, bf16[256,256]{1,0:T(8,128)(2,1)}, bf16[256,256]{1,0:T(8,128)(2,1)}, bf16[256,256]{1,0:T(8,128)(2,1)}, bf16[256,256...) custom-call(bf16[256,256]{1,0:T(8,128)(2,1)} %q_hbm.1, bf16[256,256]{1,0:T(8,128)(2,1)} %k_hbm.1, ...), custom_call_target="tpu_custom_call" | custom-call | tf_op jit(solution)/shard_map/hyena/pallas_call | solution.py:390
  50.0 2.1 %finish.1 = (bf16[256,256]{1,0:T(8,128)(2,1)}, bf16[256,256]{1,0:T(8,128)(2,1)}, bf16[256,256]{1,0:T(8,128)(2,1)}, bf16[256,256]{1,0:T(8,128)(2,1)}, f32[256,256...) custom-call(bf16[256,256]{1,0:T(8,128)(2,1)} %get-tuple-element.21.refs_0_, ...), custom_call_target="tpu_custom_call" | custom-call | tf_op jit(solution)/shard_map/finish/pallas_call | solution.py:414
